TPU v7x, 512 devices: a whole 4x8x8 slice. The times are simulated.
512 devices in a mesh: outer: 64 (over y_hi, x, z), inner: 8 (over y_lo, core).
Axes of the slice: x: 4, y: 8 (y_hi: 2, y_lo: 4; y = y_hi * 4 + y_lo), z: 8, core: 2. Of those that a mesh axis runs over, the one named last changes fastest.
Arguments:
- queries: bfloat16 [262144, 768], P(('outer', 'inner')), may hold values from -6 to 6
- keys: bfloat16 [262144, 768], P(('outer', 'inner')), may hold values from -6 to 6
- values: bfloat16 [262144, 768], P(('outer', 'inner')), may hold values from -6 to 6
- offsets: int32 [12], replicated, may hold values from 0 to 7
- w_out: bfloat16 [768, 768], replicated, may hold values from -0.21875 to 0.21875
Outputs:
- mixed: bfloat16 [262144, 768], P(('outer', 'inner'))
All inputs are finite; a program needn't handle non-finite values.
Results may differ from a plain program's by a relative error of at most 0.0056.
Values may be sent and summed in bfloat16 or wider, within the bound.
A program may use at most 64 MiB of HBM per device.

v0:
```python
import math

import jax
import jax.numpy as jnp
from jax import lax
from jax.sharding import PartitionSpec as P

LOCAL_SPAN = 256
PICKED_TOKENS = 512
LOG_G2 = 3
LEVEL_TWO_GROUPS = 8


NEG = -1e30


def swapped(shard, axis, distance):
    return lax.ppermute(shard, axis, [(i, i ^ 1 << distance) for i in range(lax.axis_size(axis))])


def head_mask(dilation_step, offsets):
    return jnp.arange(dilation_step, dtype=jnp.int32)[:, None] == offsets[None, :]


def pick(field, dilation_step, wide_mask):
    count, width = field.shape
    grid = field.reshape(count // dilation_step, dilation_step, width)
    return jnp.sum(jnp.where(wide_mask[None], grid, jnp.zeros((), field.dtype)), axis=1)


def spread(vals, dilation_step, mask, fill):
    wide = jnp.where(mask[None], vals[:, None, :], jnp.asarray(fill, jnp.float32))
    return wide.reshape(vals.shape[0] * dilation_step, vals.shape[1])


def attend(q_sel, rows, heads):
    count, width = q_sel.shape
    depth = width // heads
    scale = 1.0 / math.sqrt(depth)
    query = q_sel.reshape(count, heads, depth)
    key_rows = rows[0].reshape(rows.shape[1], heads, depth)
    value_rows = rows[1].reshape(rows.shape[1], heads, depth)
    scores = jnp.einsum("phd,shd->hps", query, key_rows, preferred_element_type=jnp.float32) * scale
    top = jnp.max(scores, axis=2)
    expo = jnp.exp(scores - top[:, :, None])
    total = jnp.sum(expo, axis=2)
    weights = expo.astype(jnp.bfloat16)
    numer = jnp.einsum("hps,shd->phd", weights, value_rows, preferred_element_type=jnp.float32)
    return (top.T, total.T, numer.reshape(count, width))


def local_level(queries, keys, values, heads):
    token_rows, width = queries.shape
    depth = width // heads
    segments = token_rows // LOCAL_SPAN
    shape = (segments, LOCAL_SPAN, heads, depth)
    scale = 1.0 / math.sqrt(depth)
    scores = (
        jnp.einsum(
            "bphd,bshd->bhps",
            queries.reshape(shape),
            keys.reshape(shape),
            preferred_element_type=jnp.float32,
        )
        * scale
    )
    top = jnp.max(scores, axis=3)
    expo = jnp.exp(scores - top[:, :, :, None])
    total = jnp.sum(expo, axis=3)
    weights = expo.astype(jnp.bfloat16)
    numer = jnp.einsum(
        "bhps,bshd->bphd", weights, values.reshape(shape), preferred_element_type=jnp.float32
    )
    top = jnp.transpose(top, (0, 2, 1)).reshape(token_rows, heads)
    total = jnp.transpose(total, (0, 2, 1)).reshape(token_rows, heads)
    return (top, total, numer.reshape(token_rows, width))


def combine(parts, depth):
    peak = parts[0][0]
    for part in parts[1:]:
        peak = jnp.maximum(peak, part[0])
    denom = jnp.zeros(peak.shape, jnp.float32)
    summed = jnp.zeros(parts[0][2].shape, jnp.float32)
    for top, total, numer in parts:
        factor = jnp.exp(top - peak)
        denom = denom + factor * total
        summed = summed + jnp.repeat(factor, depth, axis=1) * numer
    return summed / jnp.repeat(denom, depth, axis=1)


def shards(queries, keys, values, offsets, w_out):
    token_rows, width = queries.shape
    heads = offsets.shape[0]
    depth = width // heads
    inner_count = lax.axis_size("inner")
    outer_count = lax.axis_size("outer")
    dilate_level_one = inner_count * token_rows // PICKED_TOKENS
    dilate_level_two = LEVEL_TWO_GROUPS * dilate_level_one
    dilate_level_three = outer_count * inner_count * token_rows // PICKED_TOKENS

    def local_rows(dilation_step):
        wide_mask = jnp.repeat(head_mask(dilation_step, offsets), depth, axis=1)
        return jnp.stack(
            [pick(keys, dilation_step, wide_mask), pick(values, dilation_step, wide_mask)]
        )

    first_level = local_rows(dilate_level_one)
    second_level = local_rows(dilate_level_two)
    third_level = local_rows(dilate_level_three)
    first_level, second_level, third_level = (
        lax.all_gather(first_level, "inner", axis=1, tiled=True),
        lax.all_gather(second_level, "inner", axis=1, tiled=True),
        lax.all_gather(third_level, "inner", axis=1, tiled=True),
    )
    for bit in range(LOG_G2):
        partner = swapped(second_level, "outer", bit)
        second_level = jnp.concatenate([second_level, partner], axis=1)
    third_level = lax.all_gather(third_level, "outer", axis=1, tiled=True)
    levels = [local_level(queries, keys, values, heads)]
    for dilation_step, gathered_rows in (
        (dilate_level_one, first_level),
        (dilate_level_two, second_level),
        (dilate_level_three, third_level),
    ):
        narrow_mask = head_mask(dilation_step, offsets)
        wide_mask = jnp.repeat(narrow_mask, depth, axis=1)
        top, total, numer = attend(pick(queries, dilation_step, wide_mask), gathered_rows, heads)
        levels.append(
            (
                spread(top, dilation_step, narrow_mask, NEG),
                spread(total, dilation_step, narrow_mask, 0.0),
                spread(numer, dilation_step, wide_mask, 0.0),
            )
        )
    attended = combine(levels, depth).astype(jnp.bfloat16)
    return jnp.dot(attended, w_out, preferred_element_type=jnp.float32).astype(jnp.bfloat16)


def solution(mesh):
    placed = (
        P(("outer", "inner"), None),
        P(("outer", "inner"), None),
        P(("outer", "inner"), None),
        P(),
        P(),
    )
    return jax.shard_map(
        shards, mesh=mesh, in_specs=placed, out_specs=P(("outer", "inner"), None), check_vma=False
    )
```

profile of v0, /device:TPU:8, one launch (start us, length us, event | category | flops | bytes accessed | tf_op | source)
XLA Modules:
  0.0 241.6 jit_solution(3210843022270039897)
XLA Ops:
  8.2 3.5 %fusion.24 = (bf16[64,768]{1,0:T(8,128)(2,1)}, bf16[64,768]{1,0:T(8,128)(2,1)S(1)}, bf16[64,768]{1,0:T(8,128)(2,1)S(1)}) fusion(bf16[512,768]{1,0:T(8,128)(2,1)} %param.5, pred[8,768]{1,0:T(8,128)(4,1)S(1)} %broadcast_in_dim.241, bf16[512,768]{1,0:T(8,128)(2,1)} %param.6, bf16[512,768]{1,0:T(8,128)(2,1)} %param.7), kind=kLoop, calls=%fused_computation.39 | loop fusion | flops 2211840 | bytes 2660352 | tf_op jit(solution)/shard_map/reduce_sum | solution.py:28
  13.6 1.7 broadcast_in_dim.248
  15.3 1.9 select_reduce_fusion.2
  17.2 17.4 %all_gather.13 = bf16[2,64,768]{2,0,1:T(2,128)(2,1)} all-gather(bf16[2,8,768]{2,0,1:T(2,128)(2,1)S(1)} %copy.158), channel_id=1, replica_groups=mesh['outer'=64,'inner'=8] {'inner'}, dimensions={1}, use_global_device_ids=true | all-gather | bytes 221184 | tf_op jit(solution)/shard_map/all_gather | solution.py:113
  34.6 2.3 collective-permute-start
  38.2 1.4 copy.163
  39.6 1.2 fusion.20
  40.9 15.0 %all_gather.14 = bf16[2,8,768]{2,0,1:T(2,128)(2,1)} all-gather(bf16[2,1,768]{2,0,1:T(2,128)(2,1)S(1)} %copy.164), channel_id=1, replica_groups=mesh['outer'=64,'inner'=8] {'inner'}, dimensions={1}, use_global_device_ids=true | all-gather | bytes 27648 | tf_op jit(solution)/shard_map/all_gather | solution.py:114
  55.9 1.1 reshape.246
  57.1 1.1 reshape.247
  58.2 1.5 pad_maximum_fusion.1
  59.7 6.3 %collective-permute-start.1 = (bf16[2,128,768]{2,0,1:T(2,128)(2,1)S(1)}, bf16[2,128,768]{2,0,1:T(2,128)(2,1)S(1)}, u32[]{:S(2)}, u32[]{:S(2)}) collective-permute-start(bf16[2,128,768]{2,0,1:T(2,128)(2,1)S(1)} %pad_maximum_fusion.1), channel_id=1, source_target_pairs={{0,16},{8,24},{16,0},{24,8},{32,48},{40,56},{48,32},{56,40},{64,80... | collective-permute-start | bytes 1179656 | tf_op jit(solution)/shard_map/ppermute | solution.py:18
  66.1 2.2 multiply_reduce_fusion
  68.3 15.3 %collective-permute-done.1 = bf16[2,128,768]{2,0,1:T(2,128)(2,1)S(1)} collective-permute-done((bf16[2,128,768]{2,0,1:T(2,128)(2,1)S(1)}, bf16[2,128,768]{2,0,1:T(2,128)(2,1)S(1)}, u32[]{:S(2)}, u32[]{:S(2)}) %collective-permute-start.1) | collective-permute-done | bytes 393248 | tf_op jit(solution)/shard_map/ppermute | solution.py:18
  83.6 3.1 %pad_maximum_fusion = bf16[2,256,768]{2,0,1:T(2,128)(2,1)} fusion(bf16[2,128,768]{2,0,1:T(2,128)(2,1)S(1)} %collective-permute-done.1, bf16[2,64,768]{2,0,1:T(2,128)(2,1)} %collective-permute-done, bf16[2,64,768]{2,0,1:T(2,128)(2,1)} %all_gather.13), kind=kLoop, calls=%fused_computation.33 | loop fusion | flops 786432 | bytes 1572864 | tf_op jit(solution)/shard_map/concatenate | solution.py:118
  86.7 9.0 %collective-permute-start.2 = (bf16[2,256,768]{2,0,1:T(2,128)(2,1)}, bf16[2,256,768]{2,0,1:T(2,128)(2,1)}, u32[]{:S(2)}, u32[]{:S(2)}) collective-permute-start(bf16[2,256,768]{2,0,1:T(2,128)(2,1)} %pad_maximum_fusion), channel_id=1, source_target_pairs={{0,32},{8,40},{16,48},{24,56},{32,0},{40,8},{48,16},{56,24},{64,96... | collective-permute-start | bytes 2359304 | tf_op jit(solution)/shard_map/ppermute | solution.py:18
  95.7 1.2 fusion.12
  97.5 1.4 reshape.254
  98.9 1.8 reshape.250
  100.7 1.3 reshape.271
  103.5 1.2 copy.169
  104.7 1.3 copy.186
  106.8 1.1 fusion
  108.6 1.1 constant_dynamic-update-slice_fusion.3
  109.6 1.1 constant_dynamic-update-slice_fusion.2
  111.1 19.5 %collective-permute-done.2 = bf16[2,256,768]{2,0,1:T(2,128)(2,1)} collective-permute-done((bf16[2,256,768]{2,0,1:T(2,128)(2,1)}, bf16[2,256,768]{2,0,1:T(2,128)(2,1)}, u32[]{:S(2)}, u32[]{:S(2)}) %collective-permute-start.2) | collective-permute-done | bytes 786464 | tf_op jit(solution)/shard_map/ppermute | solution.py:18
  130.5 1.8 constant_dynamic-update-slice_fusion
  132.3 3.3 %fusion.49 = (bf16[1,512,768]{2,0,1:T(2,128)(2,1)}, bf16[1,512,768]{2,0,1:T(2,128)(2,1)S(1)}) fusion(bf16[2,512,768]{2,0,1:T(2,128)(2,1)S(1)} %constant_dynamic-update-slice_fusion), kind=kLoop, calls=%fused_computation.92 | loop fusion | bytes 3145728 | tf_op jit(solution)/shard_map/slice | solution.py:41
  135.6 3.4 %copy.159 = bf16[1,512,768]{1,2,0:T(8,128)(2,1)S(1)} copy(bf16[1,512,768]{2,0,1:T(2,128)(2,1)} %get-tuple-element.23) | data formatting | bytes 1572864 | tf_op jit(solution)/shard_map/slice | solution.py:41
  139.1 1.0 fusion.50
  143.1 2.0 copy.173
  145.0 1.3 convolution_bitcast_fusion
  147.4 1.6 copy.175
  149.0 5.3 %fusion.48 = (bf16[1,512,768]{2,0,1:T(2,128)(2,1)S(1)}, bf16[1,512,768]{2,0,1:T(2,128)(2,1)}) fusion(bf16[2,512,768]{2,0,1:T(2,128)(2,1)} %all-gather.3.cloned.1.call-done), kind=kLoop, calls=%fused_computation.91 | loop fusion | bytes 3145728 | tf_op jit(solution)/shard_map/slice | solution.py:41
  154.3 2.0 copy.155
  156.3 1.4 fusion.51
  160.1 3.4 %copy.170 = bf16[1,512,768]{1,2,0:T(8,128)(2,1)S(1)} copy(bf16[1,512,768]{2,0,1:T(2,128)(2,1)} %get-tuple-element.22) | data formatting | bytes 1572864 | tf_op jit(solution)/shard_map/slice | solution.py:42
  163.6 1.2 fusion.17
  164.8 1.1 copy.171
  166.8 1.7 copy.172
  168.5 47.2 %all-gather.5.cloned.1.call-done = bf16[2,512,768]{2,0,1:T(2,128)(2,1)} async-done(((bf16[2,8,768]{2,0,1:T(2,128)(2,1)}), bf16[2,512,768]{2,0,1:T(2,128)(2,1)}) %all-gather.5.cloned.1.call-update) | async-done | bytes 1572880 | tf_op jit(solution)/shard_map/all_gather | solution.py:119
  215.7 5.3 %fusion.47 = (bf16[1,512,768]{2,0,1:T(2,128)(2,1)}, bf16[1,512,768]{2,0,1:T(2,128)(2,1)S(1)}) fusion(bf16[2,512,768]{2,0,1:T(2,128)(2,1)} %all-gather.5.cloned.1.call-done), kind=kLoop, calls=%fused_computation.90 | loop fusion | bytes 3145728 | tf_op jit(solution)/shard_map/slice | solution.py:42
  221.0 4.7 %copy.184 = bf16[1,512,768]{1,2,0:T(8,128)(2,1)} copy(bf16[1,512,768]{2,0,1:T(2,128)(2,1)} %get-tuple-element.19) | data formatting | bytes 1572864
  225.6 2.0 copy.183
  228.2 1.4 fusion.41
  229.7 1.0 multiply_add_fusion
  230.7 2.4 %fusion.11 = bf16[512,768]{0,1:T(8,128)(2,1)S(1)} fusion(f32[512,768]{0,1:T(8,128)} %copy.175, f32[512,768]{0,1:T(8,128)} %copy.172, f32[512,768]{0,1:T(8,128)S(1)} %bitcast.156, f32[512,12]{0,1:T(8,128)S(1)} %get-tuple-element.14, f32[768]{0:T(1024)S(1)} %broadcast_in_dim.267, f32[512,12]{0,1:T(8,128)S(1)} %get-tuple-element.18, ...), kind=kLoop, calls=%fused_computation.21 | loop fusion | flops 3932160 | bytes 5637120 | tf_op jit(solution)/shard_map/convert_element_type | solution.py:136
  233.1 1.7 convolution_convert_fusion
  (85 shorter events, 16.8 us)
Async XLA Ops:
  6.5 226.5 %copy-start = (bf16[768,768]{1,0:T(8,128)(2,1)S(1)}, bf16[768,768]{1,0:T(8,128)(2,1)}, u32[]{:S(2)}) copy-start(bf16[768,768]{1,0:T(8,128)(2,1)} %param.9) | copy-start | bytes 3538948
  6.5 142.5 %all-gather.3.cloned.1.call-start = ((), (), s32[]{:S(2)}) async-start(), calls=%async_computation | async-start | bytes 1769472 | tf_op jit(solution)/shard_map/all_gather | solution.py:112
  7.4 0.5 copy-start.15
  8.2 4.4 %copy-start.13 = (pred[8,768]{1,0:T(8,128)(4,1)}, pred[8,768]{1,0:T(8,128)(4,1)S(1)}, u32[]{:S(2)}) copy-start(pred[8,768]{1,0:T(8,128)(4,1)S(1)} %broadcast_in_dim.241) | copy-start | bytes 18436
  8.2 4.5 %copy-start.17 = (s32[12]{0:T(128)S(1)}, s32[12]{0:T(128)}, u32[]{:S(2)}) copy-start(s32[12]{0:T(128)} %param.8) | copy-start | bytes 148
  8.2 7.1 %copy-start.3 = (bf16[512,768]{1,0:T(8,128)(2,1)S(1)}, bf16[512,768]{1,0:T(8,128)(2,1)}, u32[]{:S(2)}) copy-start(bf16[512,768]{1,0:T(8,128)(2,1)} %param.5) | copy-start | bytes 2359300
  8.2 7.1 %copy-start.4 = (bf16[512,768]{1,0:T(8,128)(2,1)S(1)}, bf16[512,768]{1,0:T(8,128)(2,1)}, u32[]{:S(2)}) copy-start(bf16[512,768]{1,0:T(8,128)(2,1)} %param.6) | copy-start | bytes 2359300
  8.2 7.1 %copy-start.5 = (bf16[512,768]{1,0:T(8,128)(2,1)S(1)}, bf16[512,768]{1,0:T(8,128)(2,1)}, u32[]{:S(2)}) copy-start(bf16[512,768]{1,0:T(8,128)(2,1)} %param.7) | copy-start | bytes 2359300
  12.6 203.0 %all-gather.5.cloned.1.call-start = ((), (), s32[]{:S(2)}) async-start(), calls=%async_computation.1 | async-start | bytes 1597440 | tf_op jit(solution)/shard_map/all_gather | solution.py:119
  34.6 23.6 %collective-permute-start = (bf16[2,64,768]{2,0,1:T(2,128)(2,1)}, bf16[2,64,768]{2,0,1:T(2,128)(2,1)}, u32[]{:S(2)}, u32[]{:S(2)}) collective-permute-start(bf16[2,64,768]{2,0,1:T(2,128)(2,1)} %all_gather.13), channel_id=1, source_target_pairs={{0,8},{8,0},{16,24},{24,16},{32,40},{40,32},{48,56},{56,48},{64,72... | collective-permute-start | bytes 589832 | tf_op jit(solution)/shard_map/ppermute | solution.py:18
  57.1 8.9 %copy-start.7 = (bf16[2,256,12,64]{1,0,3,2:T(2,128)(2,1)S(1)}, bf16[2,256,12,64]{1,0,3,2:T(2,128)(2,1)}, u32[]{:S(2)}) copy-start(bf16[2,256,12,64]{1,0,3,2:T(2,128)(2,1)} %reshape.246) | copy-start | bytes 2359300
  59.7 23.8 %collective-permute-start.1 = (bf16[2,128,768]{2,0,1:T(2,128)(2,1)S(1)}, bf16[2,128,768]{2,0,1:T(2,128)(2,1)S(1)}, u32[]{:S(2)}, u32[]{:S(2)}) collective-permute-start(bf16[2,128,768]{2,0,1:T(2,128)(2,1)S(1)} %pad_maximum_fusion.1), channel_id=1, source_target_pairs={{0,16},{8,24},{16,0},{24,8},{32,48},{40,56},{48,32},{56,40},{64,80... | collective-permute-start | bytes 1179656 | tf_op jit(solution)/shard_map/ppermute | solution.py:18
  68.3 27.4 %copy-start.1 = (f32[2,12,256,256]{2,3,1,0:T(8,128)}, f32[2,12,256,256]{2,3,1,0:T(8,128)S(1)}, u32[]{:S(2)}) copy-start(f32[2,12,256,256]{2,3,1,0:T(8,128)S(1)} %get-tuple-element.36) | copy-start | bytes 18874372
  68.3 27.4 %copy-start.11 = (f32[2,12,256]{2,1,0:T(8,128)}, f32[2,12,256]{2,1,0:T(8,128)S(1)}, u32[]{:S(2)}) copy-start(f32[2,12,256]{2,1,0:T(8,128)S(1)} %get-tuple-element.35) | copy-start | bytes 73732
  83.6 12.1 %copy-start.9 = (bf16[2,128,768]{2,0,1:T(2,128)(2,1)}, bf16[2,128,768]{2,0,1:T(2,128)(2,1)S(1)}, u32[]{:S(2)}) copy-start(bf16[2,128,768]{2,0,1:T(2,128)(2,1)S(1)} %collective-permute-done.1) | copy-start | bytes 1179652
  86.7 43.8 %collective-permute-start.2 = (bf16[2,256,768]{2,0,1:T(2,128)(2,1)}, bf16[2,256,768]{2,0,1:T(2,128)(2,1)}, u32[]{:S(2)}, u32[]{:S(2)}) collective-permute-start(bf16[2,256,768]{2,0,1:T(2,128)(2,1)} %pad_maximum_fusion), channel_id=1, source_target_pairs={{0,32},{8,40},{16,48},{24,56},{32,0},{40,8},{48,16},{56,24},{64,96... | collective-permute-start | bytes 2359304 | tf_op jit(solution)/shard_map/ppermute | solution.py:18
  102.8 3.2 %copy-start.12 = (f32[2,12,256]{2,1,0:T(8,128)S(1)}, f32[2,12,256]{2,1,0:T(8,128)}, u32[]{:S(2)}) copy-start(f32[2,12,256]{2,1,0:T(8,128)} %copy-done.11) | copy-start | bytes 73732
  103.5 3.4 %copy-start.2 = (f32[2,12,256,256]{2,3,1,0:T(8,128)S(1)}, f32[2,12,256,256]{2,3,1,0:T(8,128)}, u32[]{:S(2)}) copy-start(f32[2,12,256,256]{2,3,1,0:T(8,128)} %copy-done.1) | copy-start | bytes 18874372
  106.8 3.9 %copy-start.10 = (bf16[2,128,768]{2,0,1:T(2,128)(2,1)S(1)}, bf16[2,128,768]{2,0,1:T(2,128)(2,1)}, u32[]{:S(2)}) copy-start(bf16[2,128,768]{2,0,1:T(2,128)(2,1)} %copy-done.9) | copy-start | bytes 1179652
  140.1 0.7 copy-start.8
  156.2 1.9 copy-start.16
  225.6 2.0 copy-start.14
  227.6 3.0 %copy-start.6 = (f32[96,8,2,256]{3,1,2,0:T(8,128)S(1)}, f32[96,8,2,256]{3,1,2,0:T(8,128)}, u32[]{:S(2)}) copy-start(f32[96,8,2,256]{3,1,2,0:T(8,128)} %copy.186) | copy-start | bytes 4718596
Sparse Core Ops, SparseCore 0:
  12.8 41.9 all-gather.2
  59.4 156.2 all-gather.4
where the time goes:
time: 243 us; the launch traced here: 242 us
  waiting for transfers between devices  82 us (34%)
  local copies, waits for them, and re-layouts  63.1 us (26%)
  blocking collectives  32.4 us (13%)
  other arithmetic  21.1 us (9%)
  starting transfers between devices  17.6 us (7%)
  between operations  13.8 us (6%)
  matrix products  11.6 us (5%)
    all_gather x1, waiting for transfers between devices, shards(): third_level = lax.all_gather(third_level, 'outer', axis=1, tiled=True)  47.2 us
    ppermute x3, waiting for transfers between devices, swapped(): lax.ppermute(shard, axis, [(i, i ^ 1 << distance) for i in range(lax.axis...  34.8 us
    ppermute x3, starting transfers between devices, swapped(): lax.ppermute(shard, axis, [(i, i ^ 1 << distance) for i in range(lax.axis...  17.6 us
    all_gather x1, blocking collectives, shards(): lax.all_gather(second_level, 'inner', axis=1, tiled=True)  17.4 us
    unnamed x49, local copies, waits for them, and re-layouts  15.7 us
    all_gather x1, blocking collectives, shards(): lax.all_gather(third_level, 'inner', axis=1, tiled=True)  15 us
    slice x4, local copies, waits for them, and re-layouts, attend(): key_rows = rows[0].reshape(rows.shape[1], heads, depth)  14 us
    slice x3, local copies, waits for them, and re-layouts, attend(): value_rows = rows[1].reshape(rows.shape[1], heads, depth)  10.7 us
  transfers between devices with their start and end apart: 5, of which 3 were waited for; matrix products, arithmetic and copies ran while one was open for 29% of the time, Pallas kernels for 0%

commit v1 on v0

v1 whole, which is shorter than its diff:
```python
import math

import jax
import jax.numpy as jnp
from jax import lax
from jax.experimental import pallas as pl
from jax.experimental.pallas import tpu as pltpu
from jax.sharding import PartitionSpec as P

MESH = pl.DeviceIdType.MESH
F32, BF16 = jnp.float32, jnp.bfloat16
LANES = 128
HALF = 64
SPAN = 256
TOK = 512
PICK = 64
PAIRS = 6
COEF = 0.125 * math.log2(math.e)


def iota(shape, dim):
    return lax.broadcasted_iota(jnp.int32, shape, dim)


def nn(a, b):
    return lax.dot_general(a, b, (((1,), (0,)), ((), ())), preferred_element_type=F32)


def nt(a, b):
    return lax.dot_general(a, b, (((1,), (1,)), ((), ())), preferred_element_type=F32)


def tn(a, b):
    return lax.dot_general(a, b, (((0,), (0,)), ((), ())), preferred_element_type=F32)


def onehot(cond):
    return jnp.where(cond, jnp.float32(1), jnp.float32(0)).astype(BF16)


def eye(n):
    return onehot(iota((n, n), 0) == iota((n, n), 1))


def stacked(q):
    low = iota(q.shape, 1) < HALF
    wide = q.astype(F32)
    return jnp.concatenate([jnp.where(low, wide, 0.0), jnp.where(low, 0.0, wide)], axis=0).astype(BF16)


def split3(x):
    hi = x.astype(BF16).astype(F32)
    rest = x - hi
    mid = rest.astype(BF16).astype(F32)
    return hi, mid, rest - mid


def flipped(v):
    up = nt(eye(LANES), v)
    return jnp.concatenate([up, jnp.ones((16, v.shape[0]), F32)], axis=0).astype(BF16)


def attend_t(keys, queries, v_up):
    s = nt(keys, queries)
    top = jnp.max(s, axis=0, keepdims=True)
    w = jnp.exp2((s - top) * COEF).astype(BF16)
    return top, nn(v_up, w)


def kernel(off_ref, q_ref, k_ref, v_ref, out_ref, pick2, pick1, buf1, buf2, buf3, three, ret1, got1, ret2, got2,
           spread, v_up, sel_loc, s_a1, r_a1, s_a2, r_a2, s_b, r_b, s_c, r_c, s_d, r_d, s_e, r_e, s_f, r_f):
    outer = lax.axis_index("outer")
    i = lax.axis_index("inner")
    z = lax.rem(outer, 8)
    xy = outer // 8
    pair = i - 1
    owner = jnp.logical_and(i >= 1, i <= PAIRS)

    def of_inner(k):
        return (outer, lax.rem(i + k, 8))

    def of_z(k):
        return (xy * 8 + lax.rem(z + k, 8), i)

    def of_xy(k):
        return (lax.rem(xy + k, 8) * 8 + z, i)

    barrier = pltpu.get_barrier_semaphore()
    for k in range(1, 8):
        for at in (of_inner, of_z, of_xy):
            pl.semaphore_signal(barrier, inc=1, device_id=at(k), device_id_type=MESH)

    def cols(p):
        return slice(p * LANES, (p + 1) * LANES)

    def copy(src, dst, s, r, to):
        return pltpu.make_async_remote_copy(src_ref=src, dst_ref=dst, send_sem=s, recv_sem=r, device_id=to,
                                            device_id_type=MESH)

    low8 = iota((8, LANES), 1) < HALF
    for p in range(PAIRS):
        row = iota((16, TOK), 0)
        offs = jnp.where(row < 8, off_ref[2 * p], off_ref[2 * p + 1])
        hot = onehot(iota((16, TOK), 1) == PICK * lax.rem(row, 8) + offs)
        rows = []
        for ref in (k_ref, v_ref):
            got = nn(hot, ref[:, cols(p)])
            rows.append(jnp.where(low8, got[0:8], got[8:16]))
        pick2[p] = jnp.concatenate(rows, axis=0).astype(BF16)

    low64 = iota((PICK, LANES), 1) < HALF
    for p in range(PAIRS):
        row = iota((LANES, TOK), 0)
        offs = jnp.where(row < HALF, off_ref[2 * p], off_ref[2 * p + 1])
        hot = onehot(iota((LANES, TOK), 1) == 8 * lax.rem(row, HALF) + offs)
        for n, ref in enumerate((k_ref, v_ref, q_ref)):
            got = nn(hot, ref[:, cols(p)])
            pick1[p, n * PICK : (n + 1) * PICK] = jnp.where(low64, got[0:64], got[64:128]).astype(BF16)

    pl.semaphore_wait(barrier, 21)

    def send_a1(p):
        return copy(pick2.at[p], buf2.at[z, i], s_a1.at[p], r_a1.at[i], (outer, p + 1))

    def send_a2(p):
        return copy(pick1.at[p], buf1.at[i], s_a2.at[p], r_a2.at[i], (outer, p + 1))

    for p in range(PAIRS):
        @pl.when(i != p + 1)
        def _(p=p):
            send_a1(p).start()

        @pl.when(i == p + 1)
        def _(p=p):
            buf2[z, i] = pick2[p]

    for p in range(PAIRS):
        @pl.when(i != p + 1)
        def _(p=p):
            send_a2(p).start()

        @pl.when(i == p + 1)
        def _(p=p):
            buf1[i] = pick1[p]

    def local(p):
        v_up[p] = flipped(v_ref[:, cols(p)])
        for g in range(TOK // SPAN):
            rows = slice(g * SPAN, (g + 1) * SPAN)
            _, o = attend_t(k_ref[rows, cols(p)], stacked(q_ref[rows, cols(p)]), v_up[p, :, rows])
            a = o[0:64, 0:SPAN] / o[128:129, 0:SPAN]
            b = o[64:128, 0 + SPAN : 2 * SPAN] / o[128:129, SPAN : 2 * SPAN]
            up = jnp.concatenate([a, b], axis=0).astype(BF16)
            flat = nt(eye(SPAN), up)
            offs = jnp.where(iota((SPAN, LANES), 1) < HALF, off_ref[2 * p], off_ref[2 * p + 1])
            on = lax.rem(iota((SPAN, LANES), 0), 8) == offs
            out_ref[rows, cols(p)] = jnp.where(on, 0.0, flat).astype(BF16)

    lane = iota((1, LANES), 1)

    def local_selected(p):
        qs = stacked(pick1[p, 2 * PICK : 3 * PICK])
        parts = []
        for g in range(TOK // SPAN):
            rows = slice(g * SPAN, (g + 1) * SPAN)
            parts.append(attend_t(k_ref[rows, cols(p)], qs, v_up[p, :, rows]))
        first = lax.rem(lane, HALF) < PICK // 2
        top = jnp.where(first, parts[0][0], parts[1][0])
        o = jnp.where(first, parts[0][1], parts[1][1])
        sel_loc[p, 0:64] = jnp.where(lane < HALF, o[0:64], o[64:128])
        sel_loc[p, 64:72] = jnp.broadcast_to(top, (8, LANES))
        sel_loc[p, 72:80] = jnp.broadcast_to(o[128:129], (8, LANES))
        col = iota((TOK, LANES), 1)
        offs = jnp.where(col < HALF, off_ref[2 * p], off_ref[2 * p + 1])
        spread[p] = onehot(iota((TOK, LANES), 0) == 8 * lax.rem(col, HALF) + offs)

    def z_send(buf, s, r, k):
        return copy(buf.at[z], buf.at[z], s.at[k], r.at[z], of_z(k))

    def z_recv(buf, s, r, k):
        other = lax.rem(z + k, 8)
        return copy(buf.at[other], buf.at[other], s.at[k], r.at[other], of_z(k))

    local(0)
    local(1)

    @pl.when(owner)
    def _():
        for k in range(1, 8):
            src = lax.rem(i + k, 8)
            copy(pick2.at[0], buf2.at[z, src], s_a1.at[0], r_a1.at[src], of_inner(k)).wait_recv()
        rows = buf2[z].reshape(LANES, LANES)
        r, c = iota((16, LANES), 0), iota((16, LANES), 1)
        hot = onehot(c == 16 * lax.rem(r, 8) + 8 * (r // 8))
        buf3[xy, z] = nn(hot, rows).astype(BF16)
        for k in (4, 3, 5, 2, 6, 1, 7):
            copy(buf3.at[xy, z], buf3.at[xy, z], s_c.at[k], r_c.at[z], of_z(k)).start()
        for k in (4, 3, 5, 2, 6, 1, 7):
            z_send(buf2, s_b, r_b, k).start()

    local(2)
    local(3)

    @pl.when(owner)
    def _():
        for k in range(1, 8):
            other = lax.rem(z + k, 8)
            copy(buf3.at[xy, z], buf3.at[xy, other], s_c.at[k], r_c.at[other], of_z(k)).wait_recv()
        for k in range(1, 8):
            copy(buf3.at[xy], buf3.at[xy], s_d.at[k], r_d.at[xy], of_xy(k)).start()

    local(4)
    local(5)

    def level_one():
        keys = buf1[:, 0:PICK].reshape(8 * PICK, LANES)
        values = flipped(buf1[:, PICK : 2 * PICK].reshape(8 * PICK, LANES))
        for n in range(4):
            qs = jnp.concatenate([stacked(buf1[2 * n, 2 * PICK :]), stacked(buf1[2 * n + 1, 2 * PICK :])], axis=0)
            top, o = attend_t(keys, qs, values)
            total = o[128:129]
            parts = list(split3(top)) + list(split3(total)) + [jnp.zeros((10, 2 * LANES), F32)]
            both = lax.rem(iota((1, 2 * LANES), 1), LANES) < HALF
            whole = jnp.concatenate([jnp.where(both, o[0:64], o[64:128])] + parts, axis=0).astype(BF16)
            ret1[2 * n] = whole[:, 0:LANES]
            ret1[2 * n + 1] = whole[:, LANES:]

    def ret_send(ret, got, s, r, k):
        dst = lax.rem(i + k, 8)
        return copy(ret.at[dst], got.at[pair], s.at[k], r.at[pair], of_inner(k))

    @pl.when(owner)
    def _():
        for k in range(1, 8):
            src = lax.rem(i + k, 8)
            copy(pick1.at[0], buf1.at[src], s_a2.at[0], r_a2.at[src], of_inner(k)).wait_recv()
        level_one()
        for k in range(1, 8):
            ret_send(ret1, got1, s_e, r_e, k).start()
        got1[pair] = ret1[i]

    for p in range(PAIRS):
        local_selected(p)

    def keys_values(buf):
        wide = buf[...].reshape(64, 16, LANES).astype(F32)
        return (wide[:, 0:8].reshape(512, LANES).astype(BF16), wide[:, 8:16].reshape(512, LANES).astype(BF16))

    def attend_rows(queries, buf):
        keys, values = keys_values(buf)
        s = nt(queries, keys)
        top = jnp.max(s, axis=1, keepdims=True)
        e = jnp.exp2((s - top) * COEF)
        return top, jnp.sum(e, axis=1, keepdims=True), nn(e.astype(BF16), values)

    @pl.when(owner)
    def _():
        r, c = iota((LANES, TOK), 0), iota((LANES, TOK), 1)
        hot = onehot(c == PICK * (r // 16) + 8 * lax.rem(r, 8))
        q2 = nn(hot, buf1[:, 2 * PICK :].reshape(TOK, LANES))
        r, c = iota((LANES, LANES), 0), iota((LANES, LANES), 1)
        mine = (lax.rem(r, 16) < 8) == (c < HALF)
        q2 = jnp.where(mine, q2, 0.0).astype(BF16)
        for k in range(1, 8):
            z_recv(buf2, s_b, r_b, k).wait_recv()
        top2, total2, numer2 = attend_rows(q2, buf2)
        for k in range(1, 8):
            other = lax.rem(xy + k, 8)
            copy(buf3.at[xy], buf3.at[other], s_d.at[k], r_d.at[other], of_xy(k)).wait_recv()
        top3, total3, numer3 = attend_rows(q2, buf3)
        on = lax.rem(iota((LANES, 1), 0), 8) == 0
        peak = jnp.maximum(top2, jnp.where(on, top3, top2))
        f2 = jnp.exp2((top2 - peak) * COEF)
        f3 = jnp.where(on, jnp.exp2((jnp.where(on, top3, peak) - peak) * COEF), 0.0)
        total = f2 * total2 + f3 * total3
        whole = f2 * numer2 + f3 * numer3
        at = lax.rem(c, HALF)
        for n, x in enumerate(split3(peak) + split3(total)):
            whole = jnp.where(jnp.logical_and(jnp.logical_not(mine), at == n), x, whole)
        whole = jnp.where(jnp.logical_or(mine, at < 6), whole, 0.0)
        ret2[...] = whole.astype(BF16).reshape(8, 16, LANES)
        for k in range(1, 8):
            ret_send(ret2, got2, s_f, r_f, k).start()
        got2[pair] = ret2[i]

    for p in range(PAIRS):
        @pl.when(i != p + 1)
        def _(p=p):
            copy(ret1.at[0], got1.at[p], s_e.at[1], r_e.at[p], (outer, p + 1)).wait_recv()

    for p in range(PAIRS):
        @pl.when(i != p + 1)
        def _(p=p):
            copy(ret2.at[0], got2.at[p], s_f.at[1], r_f.at[p], (outer, p + 1)).wait_recv()

    r, c = iota((16, LANES), 0), iota((16, LANES), 1)
    hot = onehot(jnp.logical_and(r // 8 == c // HALF, lax.rem(c, HALF) == 8 * lax.rem(r, 8)))
    first = lane < HALF
    on = lax.rem(lane, 8) == 0
    for p in range(PAIRS):
        x = tn(got2[p], hot)
        numer2 = jnp.where(first, x[0:64], x[64:128])
        st = jnp.where(first, x[64:72], x[0:8])
        top2 = (st[0:1] + st[1:2]) + st[2:3]
        total2 = (st[3:4] + st[4:5]) + st[5:6]
        y = got1[p].astype(F32)
        numer1 = y[0:64]
        top1 = (y[64:65] + y[65:66]) + y[66:67]
        total1 = (y[67:68] + y[68:69]) + y[69:70]
        top0 = sel_loc[p, 64:65]
        total0 = sel_loc[p, 72:73]
        top2 = jnp.where(on, top2, top0)
        peak = jnp.maximum(jnp.maximum(top0, top1), top2)
        f0 = jnp.exp2((top0 - peak) * COEF)
        f1 = jnp.exp2((top1 - peak) * COEF)
        f2 = jnp.where(on, jnp.exp2((top2 - peak) * COEF), 0.0)
        total = f0 * total0 + f1 * total1 + f2 * total2
        done = (f0 * sel_loc[p, 0:64] + f1 * numer1 + f2 * numer2) / total
        both = jnp.concatenate([jnp.where(first, done, 0.0), jnp.where(first, 0.0, done)], axis=0).astype(BF16)
        back = nt(spread[p], both)
        out_ref[:, cols(p)] = (out_ref[:, cols(p)].astype(F32) + back).astype(BF16)

    for p in range(PAIRS):
        @pl.when(i != p + 1)
        def _(p=p):
            send_a1(p).wait_send()
            send_a2(p).wait_send()

    @pl.when(owner)
    def _():
        for k in range(1, 8):
            copy(buf3.at[xy, z], buf3.at[xy, z], s_c.at[k], r_c.at[z], of_z(k)).wait_send()
            z_send(buf2, s_b, r_b, k).wait_send()
            copy(buf3.at[xy], buf3.at[xy], s_d.at[k], r_d.at[xy], of_xy(k)).wait_send()
            ret_send(ret1, got1, s_e, r_e, k).wait_send()
            ret_send(ret2, got2, s_f, r_f, k).wait_send()


def shards(queries, keys, values, offsets, w_out):
    vmem = pl.BlockSpec(memory_space=pltpu.VMEM)
    dma = pltpu.SemaphoreType.DMA
    attended = pl.pallas_call(
        kernel,
        out_shape=jax.ShapeDtypeStruct(queries.shape, BF16),
        in_specs=[pl.BlockSpec(memory_space=pltpu.SMEM), vmem, vmem, vmem],
        out_specs=vmem,
        scratch_shapes=[
            pltpu.VMEM((PAIRS, 16, LANES), BF16),
            pltpu.VMEM((PAIRS, 3 * PICK, LANES), BF16),
            pltpu.VMEM((8, 3 * PICK, LANES), BF16),
            pltpu.VMEM((8, 8, 16, LANES), BF16),
            pltpu.VMEM((8, 8, 16, LANES), BF16),
            pltpu.VMEM((16, LANES), BF16),
            pltpu.VMEM((8, 80, LANES), BF16),
            pltpu.VMEM((PAIRS, 80, LANES), BF16),
            pltpu.VMEM((8, 16, LANES), BF16),
            pltpu.VMEM((PAIRS, 16, LANES), BF16),
            pltpu.VMEM((PAIRS, TOK, LANES), BF16),
            pltpu.VMEM((PAIRS, 144, TOK), BF16),
            pltpu.VMEM((PAIRS, 80, LANES), F32),
        ] + [dma((8,))] * 14,
        compiler_params=pltpu.CompilerParams(
            collective_id=0, has_side_effects=True, vmem_limit_bytes=48 * 1024 * 1024
        ),
    )(offsets, queries, keys, values)
    return jnp.dot(attended, w_out, preferred_element_type=F32).astype(BF16)


def solution(mesh):
    rows = P(("outer", "inner"), None)
    return jax.shard_map(
        shards, mesh=mesh, in_specs=(rows, rows, rows, P(), P()), out_specs=rows, check_vma=False
    )
```

time: 243 us -> 45.3 us (0.19)
  the two profiles are of different devices: /device:TPU:8 before, /device:TPU:1 now
where the time goes in v1:
time: 45.3 us; the launch traced here: 45.1 us
  Pallas kernels  39.2 us (87%)
  local copies, waits for them, and re-layouts  4.15 us (9%)
  matrix products  1.67 us (4%)
    pallas_call x1, Pallas kernels, shards(): pl.pallas_call(kernel, out_shape=jax.ShapeDtypeStruct(queries.shape, BF16...  39.2 us
    unnamed x10, local copies, waits for them, and re-layouts  4.15 us
    dot_general x1, matrix products, shards(): return jnp.dot(attended, w_out, preferred_element_type=F32).astype(BF16)  1.67 us

profile of v1, /device:TPU:1, one launch (start us, length us, event | category | flops | bytes accessed | tf_op | source)
XLA Modules:
  0.0 45.1 jit_solution(14178383288494106155)
XLA Ops:
  0.0 0.0 copy-start
  0.0 0.0 copy-start.1
  0.0 1.2 %copy-done.1 = bf16[512,768]{1,0:T(8,128)(2,1)S(1)} copy-done((bf16[512,768]{1,0:T(8,128)(2,1)S(1)}, bf16[512,768]{1,0:T(8,128)(2,1)}, u32[]{:S(2)}) %copy-start.1) | copy-done | bytes 786456
  1.2 0.0 copy-start.2
  1.2 1.1 %copy-done.2 = bf16[512,768]{1,0:T(8,128)(2,1)S(1)} copy-done((bf16[512,768]{1,0:T(8,128)(2,1)S(1)}, bf16[512,768]{1,0:T(8,128)(2,1)}, u32[]{:S(2)}) %copy-start.2) | copy-done | bytes 786456
  2.4 0.0 copy-start.3
  2.4 1.1 %copy-done.3 = bf16[512,768]{1,0:T(8,128)(2,1)S(1)} copy-done((bf16[512,768]{1,0:T(8,128)(2,1)S(1)}, bf16[512,768]{1,0:T(8,128)(2,1)}, u32[]{:S(2)}) %copy-start.3) | copy-done | bytes 786456
  3.5 0.0 copy-start.4
  3.5 0.7 %copy-done.4 = s32[12]{0:T(128)S(1)} copy-done((s32[12]{0:T(128)S(1)}, s32[12]{0:T(128)}, u32[]{:S(2)}) %copy-start.4) | copy-done | bytes 72
  4.2 39.2 %shard_map.55 = bf16[512,768]{1,0:T(8,128)(2,1)S(1)} custom-call(s32[12]{0:T(128)S(1)} %copy-done.4, bf16[512,768]{1,0:T(8,128)(2,1)S(1)} %copy-done.1, bf16[512,768]{1,0:T(8,128)(2,1)S(1)} %copy-done.2, bf16[512,768]{1,0:T(8,128)(2,1)S(1)} %copy-done.3), custom_call_target="tpu_custom_call" | custom-call | tf_op jit(solution)/shard_map/pallas_call | solution.py:342
  43.4 0.0 copy-done
  43.4 1.7 %convolution_convert_fusion = bf16[512,768]{1,0:T(8,128)(2,1)} fusion(bf16[512,768]{1,0:T(8,128)(2,1)S(1)} %shard_map.55, bf16[768,768]{1,0:T(8,128)(2,1)S(1)} %copy-done), kind=kOutput, calls=%fused_computation | convolution fusion | flops 604372992 | bytes 2752512 | tf_op jit(solution)/shard_map/dot_general | solution.py:366
Async XLA Ops:
  0.0 43.4 %copy-start = (bf16[768,768]{1,0:T(8,128)(2,1)S(1)}, bf16[768,768]{1,0:T(8,128)(2,1)}, u32[]{:S(2)}) copy-start(bf16[768,768]{1,0:T(8,128)(2,1)} %param.9) | copy-start | bytes 3538948
  0.0 1.2 %copy-start.1 = (bf16[512,768]{1,0:T(8,128)(2,1)S(1)}, bf16[512,768]{1,0:T(8,128)(2,1)}, u32[]{:S(2)}) copy-start(bf16[512,768]{1,0:T(8,128)(2,1)} %q_ref.1) | copy-start | bytes 2359300
  1.2 1.1 %copy-start.2 = (bf16[512,768]{1,0:T(8,128)(2,1)S(1)}, bf16[512,768]{1,0:T(8,128)(2,1)}, u32[]{:S(2)}) copy-start(bf16[512,768]{1,0:T(8,128)(2,1)} %k_ref.1) | copy-start | bytes 2359300
  2.4 1.1 %copy-start.3 = (bf16[512,768]{1,0:T(8,128)(2,1)S(1)}, bf16[512,768]{1,0:T(8,128)(2,1)}, u32[]{:S(2)}) copy-start(bf16[512,768]{1,0:T(8,128)(2,1)} %v_ref.1) | copy-start | bytes 2359300
  3.5 0.7 %copy-start.4 = (s32[12]{0:T(128)S(1)}, s32[12]{0:T(128)}, u32[]{:S(2)}) copy-start(s32[12]{0:T(128)} %off_ref.1) | copy-start | bytes 148

commit v2 on v1

v2 whole, which is shorter than its diff:
```python
import math

import jax
import jax.numpy as jnp
from jax import lax
from jax.experimental import pallas as pl
from jax.experimental.pallas import tpu as pltpu
from jax.sharding import PartitionSpec as P

MESH = pl.DeviceIdType.MESH
F32, BF16 = jnp.float32, jnp.bfloat16
LANES = 128
HALF = 64
SPAN = 256
TOK = 512
PICK = 64
PAIRS = 6
NEG = -1e30
COEF = 0.125 * math.log2(math.e)


def mod(x, n):
    return x & (n - 1)


def div(x, n):
    return x >> (n.bit_length() - 1)


def iota(shape, dim):
    return lax.broadcasted_iota(jnp.int32, shape, dim)


def nn(a, b):
    return lax.dot_general(a, b, (((1,), (0,)), ((), ())), preferred_element_type=F32)


def nt(a, b):
    return lax.dot_general(a, b, (((1,), (1,)), ((), ())), preferred_element_type=F32)


def tn(a, b):
    return lax.dot_general(a, b, (((0,), (0,)), ((), ())), preferred_element_type=F32)


def onehot(cond):
    return jnp.where(cond, jnp.float32(1), jnp.float32(0)).astype(BF16)


def eye(n):
    return onehot(iota((n, n), 0) == iota((n, n), 1))


def stacked(q):
    low = iota(q.shape, 1) < HALF
    wide = q.astype(F32)
    return jnp.concatenate([jnp.where(low, wide, 0.0), jnp.where(low, 0.0, wide)], axis=0).astype(BF16)


def split3(x):
    hi = x.astype(BF16).astype(F32)
    rest = x - hi
    mid = rest.astype(BF16).astype(F32)
    return hi, mid, rest - mid


def flipped(v):
    up = nt(eye(LANES), v)
    return jnp.concatenate([up, jnp.ones((16, v.shape[0]), F32)], axis=0).astype(BF16)


def attend_t(keys, queries, v_up):
    s = nt(keys, queries)
    top = jnp.max(s, axis=0, keepdims=True)
    w = jnp.exp2((s - top) * COEF).astype(BF16)
    return top, nn(v_up, w)


def kernel(off_ref, q_hbm, k_hbm, v_hbm, out_ref, q_ref, k_ref, v_ref, k_few, v_few, q_few, pick2, pick1, buf1, buf2,
           ret1, got1, ret2, got2, kv3, q3, part3, got3, spread, v_up, sel_loc, s_in, s_a1, r_a1, s_a2, r_a2, s_b, r_b,
           s_e, r_e, s_f, r_f, s_g, r_g, s_q, r_q, s_p, r_p):
    outer = lax.axis_index("outer")
    i = lax.axis_index("inner")
    z = mod(outer, 8)
    xy = div(outer, 8)
    far = div(outer, 32)
    cell = z * 4 + mod(xy, 4)
    ring = far * 8 + i
    pair = i - 1
    owner = jnp.logical_and(i >= 1, i <= PAIRS)
    early = z < 4
    first_pairs = jnp.maximum(PAIRS - div(3 * z + 1, 2), 0)
    second_pairs = jnp.maximum(first_pairs, 1)
    third_pairs = jnp.maximum(first_pairs, 3)

    loads = [pltpu.make_async_copy(hbm.at[:, pl.ds(0, 16)], few, s_in.at[n])
             for n, (hbm, few) in enumerate(((k_hbm, k_few), (v_hbm, v_few)))]
    loads += [pltpu.make_async_copy(q_hbm.at[0, pl.ds(0, 16)], q_few, s_in.at[2])]
    loads += [pltpu.make_async_copy(hbm, ref, s_in.at[3 + n])
              for n, (hbm, ref) in enumerate(((k_hbm, k_ref), (v_hbm, v_ref), (q_hbm, q_ref)))]
    for load in loads:
        load.start()

    def of_inner(k):
        return (outer, mod(i + k, 8))

    def of_z(k):
        return (xy * 8 + mod(z + k, 8), i)

    def at_cell(c):
        return (far * 32 + mod(c, 4) * 8 + div(c, 4), i)

    def of_cell(k):
        return at_cell(mod(cell + k, 32))

    def of_ring(k):
        at = mod(ring + k, 16)
        return (div(at, 8) * 32 + mod(outer, 32), mod(at, 8))

    barrier = pltpu.get_barrier_semaphore()
    for k in range(1, 16):
        pl.semaphore_signal(barrier, inc=1, device_id=of_ring(k), device_id_type=MESH)
    for k in range(1, 32):
        pl.semaphore_signal(barrier, inc=1, device_id=of_cell(k), device_id_type=MESH)

    def cols(p):
        if isinstance(p, int):
            return slice(p * LANES, (p + 1) * LANES)
        return pl.ds(pl.multiple_of(p * LANES, LANES), LANES)

    def rows_of(ref, g, p):
        return ref[g * 4 : (g + 1) * 4, :, cols(p)].reshape(SPAN, LANES)

    def all_of(ref, p):
        return ref[:, :, cols(p)].reshape(TOK, LANES)

    def copy(src, dst, s, r, to):
        return pltpu.make_async_remote_copy(src_ref=src, dst_ref=dst, send_sem=s, recv_sem=r, device_id=to,
                                            device_id_type=MESH)

    for load in loads[:3]:
        load.wait()

    def one_row(block):
        x = block.astype(F32)[0:8]
        at = iota((8, LANES), 0)
        rows = jnp.zeros((8, LANES), F32)
        for p in range(PAIRS):
            offs = jnp.where(iota((8, LANES), 1) < HALF, off_ref[2 * p], off_ref[2 * p + 1])
            row = jnp.sum(jnp.where(at == offs, x[:, cols(p)], 0.0), axis=0, keepdims=True)
            rows = jnp.where(at == p, row, rows)
        return rows

    kv3[ring] = jnp.concatenate([one_row(k_few[0]), one_row(v_few[0])], axis=0).astype(BF16)
    q3[cell] = one_row(q_few[...])

    low8 = iota((8, LANES), 1) < HALF
    for p in range(PAIRS):
        row = iota((16, LANES), 0)
        offs = jnp.where(row < 8, off_ref[2 * p], off_ref[2 * p + 1])
        hot = onehot(iota((16, LANES), 1) == 16 * mod(row, 8) + offs)
        rows = []
        for ref in (k_few, v_few):
            got = nn(hot, ref[:, :, cols(p)].reshape(LANES, LANES))
            rows.append(jnp.where(low8, got[0:8], got[8:16]))
        pick2[p] = jnp.concatenate(rows, axis=0).astype(BF16)

    def select(p):
        row = iota((LANES, TOK), 0)
        low = iota((PICK, LANES), 1) < HALF
        offs = jnp.where(row < HALF, off_ref[2 * p], off_ref[2 * p + 1])
        hot = onehot(iota((LANES, TOK), 1) == 8 * mod(row, HALF) + offs)
        for n, ref in enumerate((k_ref, v_ref, q_ref)):
            got = nn(hot, all_of(ref, p))
            pick1[p, n * PICK : (n + 1) * PICK] = jnp.where(low, got[0:64], got[64:128]).astype(BF16)

    def own(p):
        v_up[p] = flipped(all_of(v_ref, p))
        for g in range(TOK // SPAN):
            rows = slice(g * SPAN, (g + 1) * SPAN)
            _, o = attend_t(rows_of(k_ref, g, p), stacked(rows_of(q_ref, g, p)), v_up[p, :, rows])
            a = o[0:64, 0:SPAN] / o[128:129, 0:SPAN]
            b = o[64:128, 0 + SPAN : 2 * SPAN] / o[128:129, SPAN : 2 * SPAN]
            up = jnp.concatenate([a, b], axis=0).astype(BF16)
            flat = nt(eye(SPAN), up)
            offs = jnp.where(iota((SPAN, LANES), 1) < HALF, off_ref[2 * p], off_ref[2 * p + 1])
            on = mod(iota((SPAN, LANES), 0), 8) == offs
            out_ref[rows, cols(p)] = jnp.where(on, 0.0, flat).astype(BF16)

    lane = iota((1, LANES), 1)

    def local_selected(p):
        qs = stacked(pick1[p, 2 * PICK : 3 * PICK])
        parts = []
        for g in range(TOK // SPAN):
            rows = slice(g * SPAN, (g + 1) * SPAN)
            parts.append(attend_t(rows_of(k_ref, g, p), qs, v_up[p, :, rows]))
        first = mod(lane, HALF) < PICK // 2
        top = jnp.where(first, parts[0][0], parts[1][0])
        o = jnp.where(first, parts[0][1], parts[1][1])
        sel_loc[p, 0:64] = jnp.where(lane < HALF, o[0:64], o[64:128])
        sel_loc[p, 64:72] = jnp.broadcast_to(top, (8, LANES))
        sel_loc[p, 72:80] = jnp.broadcast_to(o[128:129], (8, LANES))
        col = iota((TOK, LANES), 1)
        offs = jnp.where(col < HALF, off_ref[2 * p], off_ref[2 * p + 1])
        spread[p] = onehot(iota((TOK, LANES), 0) == 8 * mod(col, HALF) + offs)

    def local(p):
        own(p)
        local_selected(p)

    def loop(begin, end, body):
        lax.fori_loop(begin, end, lambda p, _: (body(p), 0)[1], 0)

    @pl.when(early)
    def _():
        for load in loads[3:]:
            load.wait()
        for p in range(PAIRS):
            select(p)
        loop(0, first_pairs, local)

    pl.semaphore_wait(barrier, 46)

    def ring_copy(k):
        return copy(kv3.at[ring], kv3.at[ring], s_g.at[k], r_g.at[ring], of_ring(k))

    def query_copy(k):
        return copy(q3.at[cell], q3.at[cell], s_q.at[k], r_q.at[cell], of_cell(k))

    def part_copy(to):
        return copy(part3.at[to], got3.at[cell], s_p.at[to], r_p.at[cell], at_cell(to))

    def others(half, body):
        for k in range(16):
            at = 16 * half + mod(cell + k, 16)
            if k:
                body(at)
            else:
                pl.when(div(cell, 16) != half)(lambda: body(at))

    for k in range(1, 16):
        ring_copy(k).start()

    def send_a1(p):
        return copy(pick2.at[p], buf2.at[z, i], s_a1.at[p], r_a1.at[i], (outer, p + 1))

    def send_a2(p):
        return copy(pick1.at[p], buf1.at[i], s_a2.at[p], r_a2.at[i], (outer, p + 1))

    for p in range(PAIRS):
        @pl.when(i != p + 1)
        def _(p=p):
            send_a1(p).start()

        @pl.when(i == p + 1)
        def _(p=p):
            buf2[z, i] = pick2[p]

    for k in range(1, 32):
        query_copy(k).start()

    @pl.when(jnp.logical_not(early))
    def _():
        for load in loads[3:]:
            load.wait()
        for p in range(PAIRS):
            select(p)

    for p in range(PAIRS):
        @pl.when(i != p + 1)
        def _(p=p):
            send_a2(p).start()

        @pl.when(i == p + 1)
        def _(p=p):
            buf1[i] = pick1[p]

    def z_send(buf, s, r, k):
        return copy(buf.at[z], buf.at[z], s.at[k], r.at[z], of_z(k))

    def z_recv(buf, s, r, k):
        other = mod(z + k, 8)
        return copy(buf.at[other], buf.at[other], s.at[k], r.at[other], of_z(k))

    loop(first_pairs, second_pairs, local)

    @pl.when(owner)
    def _():
        for k in range(1, 8):
            src = mod(i + k, 8)
            copy(pick2.at[0], buf2.at[z, src], s_a1.at[0], r_a1.at[src], of_inner(k)).wait_recv()
        for k in (4, 3, 5, 2, 6, 1, 7):
            z_send(buf2, s_b, r_b, k).start()

    r, c = iota((2 * LANES, LANES), 0), iota((2 * LANES, LANES), 1)
    hot_q = onehot(jnp.logical_and(div(r, 16) == div(c, 8), div(mod(r, 16), 2) == mod(c, 8)))
    head4 = mod(r, 16)
    mine4 = mod(head4, 2) == div(c, HALF)
    key4 = div(c, 16) == div(head4, 2)
    spot4 = mod(c, HALF)

    def fourth(half, rows4):
        def arrived(at):
            copy(q3.at[at], q3.at[at], s_q.at[0], r_q.at[at], at_cell(at)).wait_recv()

        others(half, arrived)
        mine = slice(16 * half, 16 * half + 16)
        queries4 = nn(hot_q, q3[mine].reshape(LANES, LANES).astype(BF16))
        queries4 = jnp.where(mine4, queries4, 0.0).astype(BF16)
        s = jnp.where(key4, nt(queries4, rows4[0:LANES]), NEG)
        top = jnp.max(s, axis=1, keepdims=True)
        e = jnp.exp2((s - top) * COEF)
        total = jnp.sum(e, axis=1, keepdims=True)
        stats = jnp.where(spot4 == 0, top, jnp.where(spot4 == 1, total, 0.0))
        part3[mine] = jnp.where(mine4, nn(e.astype(BF16), rows4[LANES:]), stats).reshape(16, 16, LANES)
        others(half, lambda at: part_copy(at).start())

    for k in range(1, 16):
        at = mod(ring + k, 16)
        copy(kv3.at[at], kv3.at[at], s_g.at[k], r_g.at[at], of_ring(k)).wait_recv()
    r, c = iota((2 * LANES, 2 * LANES), 0), iota((2 * LANES, 2 * LANES), 1)
    hot = onehot(c == 16 * mod(r, 16) + 8 * div(r, LANES) + div(mod(r, LANES), 16))
    rows4 = nn(hot, kv3[...].reshape(2 * LANES, LANES)).astype(BF16)
    fourth(0, rows4)
    loop(second_pairs, third_pairs, local)
    fourth(1, rows4)
    got3[cell] = part3[cell]

    def level_one():
        keys = buf1[:, 0:PICK].reshape(8 * PICK, LANES)
        values = flipped(buf1[:, PICK : 2 * PICK].reshape(8 * PICK, LANES))
        for n in range(4):
            qs = jnp.concatenate([stacked(buf1[2 * n, 2 * PICK :]), stacked(buf1[2 * n + 1, 2 * PICK :])], axis=0)
            top, o = attend_t(keys, qs, values)
            total = o[128:129]
            parts = list(split3(top)) + list(split3(total)) + [jnp.zeros((10, 2 * LANES), F32)]
            both = mod(iota((1, 2 * LANES), 1), LANES) < HALF
            whole = jnp.concatenate([jnp.where(both, o[0:64], o[64:128])] + parts, axis=0).astype(BF16)
            ret1[2 * n] = whole[:, 0:LANES]
            ret1[2 * n + 1] = whole[:, LANES:]

    def ret_send(ret, got, s, r, k):
        dst = mod(i + k, 8)
        return copy(ret.at[dst], got.at[pair], s.at[k], r.at[pair], of_inner(k))

    @pl.when(owner)
    def _():
        for k in range(1, 8):
            src = mod(i + k, 8)
            copy(pick1.at[0], buf1.at[src], s_a2.at[0], r_a2.at[src], of_inner(k)).wait_recv()
        level_one()
        for k in range(1, 8):
            ret_send(ret1, got1, s_e, r_e, k).start()
        got1[pair] = ret1[i]

    def keys_values(buf):
        wide = buf[...].reshape(64, 16, LANES).astype(F32)
        return (wide[:, 0:8].reshape(512, LANES).astype(BF16), wide[:, 8:16].reshape(512, LANES).astype(BF16))

    def attend_rows(queries, buf):
        keys, values = keys_values(buf)
        s = nt(queries, keys)
        top = jnp.max(s, axis=1, keepdims=True)
        e = jnp.exp2((s - top) * COEF)
        return top, jnp.sum(e, axis=1, keepdims=True), nn(e.astype(BF16), values)

    @pl.when(owner)
    def _():
        r, c = iota((LANES, TOK), 0), iota((LANES, TOK), 1)
        hot = onehot(c == PICK * div(r, 16) + 8 * mod(r, 8))
        q2 = nn(hot, buf1[:, 2 * PICK :].reshape(TOK, LANES))
        r, c = iota((LANES, LANES), 0), iota((LANES, LANES), 1)
        mine = (mod(r, 16) < 8) == (c < HALF)
        q2 = jnp.where(mine, q2, 0.0).astype(BF16)
        for k in range(1, 8):
            z_recv(buf2, s_b, r_b, k).wait_recv()
        top2, total2, numer2 = attend_rows(q2, buf2)
        at = mod(c, HALF)
        whole = numer2
        for n, x in enumerate(split3(top2) + split3(total2)):
            whole = jnp.where(jnp.logical_and(jnp.logical_not(mine), at == n), x, whole)
        whole = jnp.where(jnp.logical_or(mine, at < 6), whole, 0.0)
        ret2[...] = whole.astype(BF16).reshape(8, 16, LANES)
        for k in range(1, 8):
            ret_send(ret2, got2, s_f, r_f, k).start()
        got2[pair] = ret2[i]

    loop(third_pairs, PAIRS, local)

    for p in range(PAIRS):
        @pl.when(i != p + 1)
        def _(p=p):
            copy(ret1.at[0], got1.at[p], s_e.at[1], r_e.at[p], (outer, p + 1)).wait_recv()

    for p in range(PAIRS):
        @pl.when(i != p + 1)
        def _(p=p):
            copy(ret2.at[0], got2.at[p], s_f.at[1], r_f.at[p], (outer, p + 1)).wait_recv()

    for k in range(1, 32):
        at = mod(cell + k, 32)
        copy(part3.at[at], got3.at[at], s_p.at[k], r_p.at[at], of_cell(k)).wait_recv()
    x = got3[...]
    lane3 = iota((32, 16, LANES), 2)
    other = mod(iota((32, 16, LANES), 1), 2) != div(lane3, HALF)
    spot = mod(lane3, HALF)
    top = jnp.max(jnp.where(jnp.logical_and(other, spot == 0), x, NEG), axis=2, keepdims=True)
    total = jnp.sum(jnp.where(jnp.logical_and(other, spot == 1), x, 0.0), axis=2, keepdims=True)
    peak = jnp.max(top, axis=0, keepdims=True)
    f = jnp.exp2((top - peak) * COEF)
    numer = jnp.sum(f * x, axis=0)
    total = jnp.sum(f * total, axis=0)
    r, c = iota((16, LANES), 0), iota((16, LANES), 1)
    mine = mod(r, 2) == div(c, HALF)
    spot = mod(c, HALF)
    for n, v in enumerate(split3(peak.reshape(16, 1)) + split3(total)):
        numer = jnp.where(jnp.logical_and(jnp.logical_not(mine), spot == n), v, numer)
    rows4 = jnp.where(jnp.logical_or(mine, spot < 6), numer, 0.0).astype(BF16)
    r, c = iota((16, PAIRS * LANES), 0), iota((16, PAIRS * LANES), 1)
    all4 = tn(rows4, onehot(jnp.logical_and(r == div(c, HALF), mod(c, HALF) == 0)))

    r, c = iota((16, LANES), 0), iota((16, LANES), 1)
    hot = onehot(jnp.logical_and(div(r, 8) == div(c, HALF), mod(c, HALF) == 8 * mod(r, 8)))
    first = lane < HALF
    on = mod(lane, 8) == 0
    on4 = mod(lane, HALF) == 0

    def unpacked(x):
        st = jnp.where(first, x[64:72], x[0:8])
        return (st[0:1] + st[1:2]) + st[2:3], (st[3:4] + st[4:5]) + st[5:6], jnp.where(first, x[0:64], x[64:128])

    for p in range(PAIRS):
        top2, total2, numer2 = unpacked(tn(got2[p], hot))
        top3, total3, numer3 = unpacked(all4[:, cols(p)])
        y = got1[p].astype(F32)
        numer1 = y[0:64]
        top1 = (y[64:65] + y[65:66]) + y[66:67]
        total1 = (y[67:68] + y[68:69]) + y[69:70]
        top0 = sel_loc[p, 64:65]
        total0 = sel_loc[p, 72:73]
        top2 = jnp.where(on, top2, top0)
        top3 = jnp.where(on4, top3, top0)
        peak = jnp.maximum(jnp.maximum(top0, top1), jnp.maximum(top2, top3))
        f0 = jnp.exp2((top0 - peak) * COEF)
        f1 = jnp.exp2((top1 - peak) * COEF)
        f2 = jnp.where(on, jnp.exp2((top2 - peak) * COEF), 0.0)
        f3 = jnp.where(on4, jnp.exp2((top3 - peak) * COEF), 0.0)
        total = f0 * total0 + f1 * total1 + f2 * total2 + f3 * total3
        done = (f0 * sel_loc[p, 0:64] + f1 * numer1 + f2 * numer2 + f3 * numer3) / total
        both = jnp.concatenate([jnp.where(first, done, 0.0), jnp.where(first, 0.0, done)], axis=0).astype(BF16)
        back = nt(spread[p], both)
        out_ref[:, cols(p)] = (out_ref[:, cols(p)].astype(F32) + back).astype(BF16)

    for k in range(1, 16):
        ring_copy(k).wait_send()
    for k in range(1, 32):
        query_copy(k).wait_send()
    for half in range(2):
        others(half, lambda at: part_copy(at).wait_send())
    for p in range(PAIRS):
        @pl.when(i != p + 1)
        def _(p=p):
            send_a1(p).wait_send()
            send_a2(p).wait_send()

    @pl.when(owner)
    def _():
        for k in range(1, 8):
            z_send(buf2, s_b, r_b, k).wait_send()
            ret_send(ret1, got1, s_e, r_e, k).wait_send()
            ret_send(ret2, got2, s_f, r_f, k).wait_send()


def shards(queries, keys, values, offsets, w_out):
    hbm = pl.BlockSpec(memory_space=pltpu.HBM)
    shape = (8, 64, queries.shape[1])
    dma = pltpu.SemaphoreType.DMA
    attended = pl.pallas_call(
        kernel,
        out_shape=jax.ShapeDtypeStruct(queries.shape, BF16),
        in_specs=[pl.BlockSpec(memory_space=pltpu.SMEM), hbm, hbm, hbm],
        out_specs=pl.BlockSpec(memory_space=pltpu.VMEM),
        scratch_shapes=[pltpu.VMEM(shape, BF16)] * 3 + [pltpu.VMEM((8, 16, shape[2]), BF16)] * 2 + [
            pltpu.VMEM((16, shape[2]), BF16),
            pltpu.VMEM((PAIRS, 16, LANES), BF16),
            pltpu.VMEM((PAIRS, 3 * PICK, LANES), BF16),
            pltpu.VMEM((8, 3 * PICK, LANES), BF16),
            pltpu.VMEM((8, 8, 16, LANES), BF16),
            pltpu.VMEM((8, 80, LANES), BF16),
            pltpu.VMEM((PAIRS, 80, LANES), BF16),
            pltpu.VMEM((8, 16, LANES), BF16),
            pltpu.VMEM((PAIRS, 16, LANES), BF16),
            pltpu.VMEM((16, 16, LANES), BF16),
            pltpu.VMEM((32, 8, LANES), F32),
            pltpu.VMEM((32, 16, LANES), F32),
            pltpu.VMEM((32, 16, LANES), F32),
            pltpu.VMEM((PAIRS, TOK, LANES), BF16),
            pltpu.VMEM((PAIRS, 144, TOK), BF16),
            pltpu.VMEM((PAIRS, 80, LANES), F32),
        ] + [dma((6,))] + [dma((8,))] * 10 + [dma((16,))] * 2 + [dma((32,))] * 4,
        compiler_params=pltpu.CompilerParams(
            collective_id=0, has_side_effects=True, vmem_limit_bytes=53 * 1024 * 1024
        ),
    )(offsets, queries.reshape(shape), keys.reshape(shape), values.reshape(shape))
    return jnp.dot(attended, w_out, preferred_element_type=F32).astype(BF16)


def solution(mesh):
    rows = P(("outer", "inner"), None)
    return jax.shard_map(
        shards, mesh=mesh, in_specs=(rows, rows, rows, P(), P()), out_specs=rows, check_vma=False
    )
```

time: 45.3 us -> 41.2 us (0.909)
  the two profiles are of different devices: /device:TPU:1 before, /device:TPU:3 now
where the time goes in v2:
time: 41.2 us; the launch traced here: 41.1 us
  Pallas kernels  38.6 us (94%)
  matrix products  1.67 us (4%)
  local copies, waits for them, and re-layouts  0.76 us (2%)
    pallas_call x1, Pallas kernels, shards(): pl.pallas_call(kernel, out_shape=jax.ShapeDtypeStruct(queries.shape, BF16...  38.6 us
    dot_general x1, matrix products, shards(): return jnp.dot(attended, w_out, preferred_element_type=F32).astype(BF16)  1.67 us

profile of v2, /device:TPU:3, one launch (start us, length us, event | category | flops | bytes accessed | tf_op | source)
XLA Modules:
  0.0 41.1 jit_solution(9907259773516580584)
XLA Ops:
  0.0 0.0 copy-start
  0.0 0.0 copy-start.1
  0.0 0.7 %copy-done.1 = s32[12]{0:T(128)S(1)} copy-done((s32[12]{0:T(128)S(1)}, s32[12]{0:T(128)}, u32[]{:S(2)}) %copy-start.1) | copy-done | bytes 72
  0.8 38.6 %shard_map.55 = bf16[512,768]{1,0:T(8,128)(2,1)S(1)} custom-call(s32[12]{0:T(128)S(1)} %copy-done.1, bf16[8,64,768]{2,1,0:T(8,128)(2,1)} %bitcast.5, bf16[8,64,768]{2,1,0:T(8,128)(2,1)} %bitcast.6, bf16[8,64,768]{2,1,0:T(8,128)(2,1)} %bitcast.7), custom_call_target="tpu_custom_call" | custom-call | tf_op jit(solution)/shard_map/pallas_call | solution.py:479
  39.4 0.0 copy-done
  39.4 1.7 %convolution_convert_fusion = bf16[512,768]{1,0:T(8,128)(2,1)} fusion(bf16[512,768]{1,0:T(8,128)(2,1)S(1)} %shard_map.55, bf16[768,768]{1,0:T(8,128)(2,1)S(1)} %copy-done), kind=kOutput, calls=%fused_computation | convolution fusion | flops 604372992 | bytes 2752512 | tf_op jit(solution)/shard_map/dot_general | solution.py:506
Async XLA Ops:
  0.0 39.4 %copy-start = (bf16[768,768]{1,0:T(8,128)(2,1)S(1)}, bf16[768,768]{1,0:T(8,128)(2,1)}, u32[]{:S(2)}) copy-start(bf16[768,768]{1,0:T(8,128)(2,1)} %param.9) | copy-start | bytes 3538948
  0.0 0.8 %copy-start.1 = (s32[12]{0:T(128)S(1)}, s32[12]{0:T(128)}, u32[]{:S(2)}) copy-start(s32[12]{0:T(128)} %off_ref.1) | copy-start | bytes 148

commit v3 on v2

--- a/solution.py
+++ b/solution.py
@@ -77,8 +77,8 @@
 
 
 def kernel(off_ref, q_hbm, k_hbm, v_hbm, out_ref, q_ref, k_ref, v_ref, k_few, v_few, q_few, pick2, pick1, buf1, buf2,
-           ret1, got1, ret2, got2, kv3, q3, part3, got3, spread, v_up, sel_loc, s_in, s_a1, r_a1, s_a2, r_a2, s_b, r_b,
-           s_e, r_e, s_f, r_f, s_g, r_g, s_q, r_q, s_p, r_p):
+           ret1, got1, ret2, got2, rows3, ring3, all3, ret3, got3, spread, v_up, sel_loc, s_in, s_a1, r_a1, s_a2, r_a2, s_b, r_b,
+           s_e, r_e, s_f, r_f, s_g, r_g, s_q, r_q, s_p, r_p, later):
     outer = lax.axis_index("outer")
     i = lax.axis_index("inner")
     z = mod(outer, 8)
@@ -86,12 +86,12 @@
     far = div(outer, 32)
     cell = z * 4 + mod(xy, 4)
     ring = far * 8 + i
+    head = far * PAIRS + i - 1
+    odd = mod(head, 2) == 1
     pair = i - 1
     owner = jnp.logical_and(i >= 1, i <= PAIRS)
-    early = z < 4
-    first_pairs = jnp.maximum(PAIRS - div(3 * z + 1, 2), 0)
-    second_pairs = jnp.maximum(first_pairs, 1)
-    third_pairs = jnp.maximum(first_pairs, 3)
+    first_pairs = jnp.clip(7 - z, 1, PAIRS)
+    second_pairs = jnp.maximum(first_pairs, 4)
 
     loads = [pltpu.make_async_copy(hbm.at[:, pl.ds(0, 16)], few, s_in.at[n])
              for n, (hbm, few) in enumerate(((k_hbm, k_few), (v_hbm, v_few)))]
@@ -120,8 +120,13 @@
     barrier = pltpu.get_barrier_semaphore()
     for k in range(1, 16):
         pl.semaphore_signal(barrier, inc=1, device_id=of_ring(k), device_id_type=MESH)
-    for k in range(1, 32):
-        pl.semaphore_signal(barrier, inc=1, device_id=of_cell(k), device_id_type=MESH)
+
+    def cells(body, chosen):
+        for k in range(1, 32):
+            at = mod(cell + k, 32)
+            pl.when(chosen(div(at, 4)))(lambda: body(at))
+
+    cells(lambda at: pl.semaphore_signal(barrier, inc=1, device_id=at_cell(at), device_id_type=MESH), lambda w: w >= z)
 
     def cols(p):
         if isinstance(p, int):
@@ -151,8 +156,14 @@
             rows = jnp.where(at == p, row, rows)
         return rows
 
-    kv3[ring] = jnp.concatenate([one_row(k_few[0]), one_row(v_few[0])], axis=0).astype(BF16)
-    q3[cell] = one_row(q_few[...])
+    key_row, value_row, query_row = one_row(k_few[0]), pltpu.roll(one_row(v_few[0]), HALF, 1), one_row(q_few[...])
+    at, low = iota((8, LANES), 0), iota((8, LANES), 1) < HALF
+    for h in range(2 * PAIRS):
+        p = div(h, 2)
+        own_half = low if h % 2 == 0 else jnp.logical_not(low)
+        both = jnp.where(own_half, key_row[p : p + 1], value_row[p : p + 1])
+        query = jnp.where(own_half, query_row[p : p + 1], 0.0)
+        rows3[h] = jnp.where(at == 0, both, jnp.where(at == 1, query, 0.0))
 
     low8 = iota((8, LANES), 1) < HALF
     for p in range(PAIRS):
@@ -212,35 +223,33 @@
     def loop(begin, end, body):
         lax.fori_loop(begin, end, lambda p, _: (body(p), 0)[1], 0)
 
-    @pl.when(early)
-    def _():
-        for load in loads[3:]:
-            load.wait()
-        for p in range(PAIRS):
-            select(p)
-        loop(0, first_pairs, local)
-
-    pl.semaphore_wait(barrier, 46)
-
-    def ring_copy(k):
-        return copy(kv3.at[ring], kv3.at[ring], s_g.at[k], r_g.at[ring], of_ring(k))
-
-    def query_copy(k):
-        return copy(q3.at[cell], q3.at[cell], s_q.at[k], r_q.at[cell], of_cell(k))
-
-    def part_copy(to):
-        return copy(part3.at[to], got3.at[cell], s_p.at[to], r_p.at[cell], at_cell(to))
-
-    def others(half, body):
-        for k in range(16):
-            at = 16 * half + mod(cell + k, 16)
-            if k:
-                body(at)
-            else:
-                pl.when(div(cell, 16) != half)(lambda: body(at))
-
-    for k in range(1, 16):
-        ring_copy(k).start()
+    pl.semaphore_wait(barrier, 15 + 3 + 4 * z)
+
+    def ring_at(g):
+        return (div(g, 8) * 32 + mod(outer, 32), mod(g, 8))
+
+    def ring_owner(h):
+        return (h // PAIRS * 32 + mod(outer, 32), h % PAIRS + 1)
+
+    def mine(h):
+        return jnp.logical_and(owner, head == h)
+
+    def ring_copy(h):
+        return copy(rows3.at[h], ring3.at[ring], s_g.at[h], r_g.at[ring], ring_owner(h))
+
+    def cell_copy(at):
+        return copy(all3.at[cell], all3.at[cell], s_q.at[at], r_q.at[cell], at_cell(at))
+
+    def back_copy(k):
+        to = mod(ring + k, 16)
+        return copy(ret3.at[to], got3.at[head], s_p.at[to], r_p.at[head], ring_at(to))
+
+    for h in range(2 * PAIRS):
+        pl.when(jnp.logical_not(mine(h)))(lambda: ring_copy(h).start())
+
+        @pl.when(mine(h))
+        def _(h=h):
+            ring3[ring] = rows3[h]
 
     def send_a1(p):
         return copy(pick2.at[p], buf2.at[z, i], s_a1.at[p], r_a1.at[i], (outer, p + 1))
@@ -257,15 +266,12 @@
         def _(p=p):
             buf2[z, i] = pick2[p]
 
-    for k in range(1, 32):
-        query_copy(k).start()
-
-    @pl.when(jnp.logical_not(early))
-    def _():
-        for load in loads[3:]:
-            load.wait()
-        for p in range(PAIRS):
-            select(p)
+    cells(lambda at: pl.semaphore_signal(later, inc=1, device_id=at_cell(at), device_id_type=MESH), lambda w: w < z)
+
+    for load in loads[3:]:
+        load.wait()
+    for p in range(PAIRS):
+        select(p)
 
     for p in range(PAIRS):
         @pl.when(i != p + 1)
@@ -283,49 +289,31 @@
         other = mod(z + k, 8)
         return copy(buf.at[other], buf.at[other], s.at[k], r.at[other], of_z(k))
 
-    loop(first_pairs, second_pairs, local)
+    loop(0, first_pairs, local)
 
     @pl.when(owner)
     def _():
+        for k in range(1, 16):
+            src = mod(ring + k, 16)
+            copy(rows3.at[0], ring3.at[src], s_g.at[0], r_g.at[src], ring_at(src)).wait_recv()
+        hot = onehot(iota((16, LANES), 1) == 8 * iota((16, LANES), 0))
+        all3[cell] = nn(hot, ring3[...].reshape(LANES, LANES).astype(BF16)).astype(BF16)
+        cells(lambda at: cell_copy(at).start(), lambda w: w <= z)
         for k in range(1, 8):
             src = mod(i + k, 8)
             copy(pick2.at[0], buf2.at[z, src], s_a1.at[0], r_a1.at[src], of_inner(k)).wait_recv()
         for k in (4, 3, 5, 2, 6, 1, 7):
-            z_send(buf2, s_b, r_b, k).start()
-
-    r, c = iota((2 * LANES, LANES), 0), iota((2 * LANES, LANES), 1)
-    hot_q = onehot(jnp.logical_and(div(r, 16) == div(c, 8), div(mod(r, 16), 2) == mod(c, 8)))
-    head4 = mod(r, 16)
-    mine4 = mod(head4, 2) == div(c, HALF)
-    key4 = div(c, 16) == div(head4, 2)
-    spot4 = mod(c, HALF)
-
-    def fourth(half, rows4):
-        def arrived(at):
-            copy(q3.at[at], q3.at[at], s_q.at[0], r_q.at[at], at_cell(at)).wait_recv()
-
-        others(half, arrived)
-        mine = slice(16 * half, 16 * half + 16)
-        queries4 = nn(hot_q, q3[mine].reshape(LANES, LANES).astype(BF16))
-        queries4 = jnp.where(mine4, queries4, 0.0).astype(BF16)
-        s = jnp.where(key4, nt(queries4, rows4[0:LANES]), NEG)
-        top = jnp.max(s, axis=1, keepdims=True)
-        e = jnp.exp2((s - top) * COEF)
-        total = jnp.sum(e, axis=1, keepdims=True)
-        stats = jnp.where(spot4 == 0, top, jnp.where(spot4 == 1, total, 0.0))
-        part3[mine] = jnp.where(mine4, nn(e.astype(BF16), rows4[LANES:]), stats).reshape(16, 16, LANES)
-        others(half, lambda at: part_copy(at).start())
-
-    for k in range(1, 16):
-        at = mod(ring + k, 16)
-        copy(kv3.at[at], kv3.at[at], s_g.at[k], r_g.at[at], of_ring(k)).wait_recv()
-    r, c = iota((2 * LANES, 2 * LANES), 0), iota((2 * LANES, 2 * LANES), 1)
-    hot = onehot(c == 16 * mod(r, 16) + 8 * div(r, LANES) + div(mod(r, LANES), 16))
-    rows4 = nn(hot, kv3[...].reshape(2 * LANES, LANES)).astype(BF16)
-    fourth(0, rows4)
-    loop(second_pairs, third_pairs, local)
-    fourth(1, rows4)
-    got3[cell] = part3[cell]
+            pl.when(mod(z + k, 8) < z)(lambda: z_send(buf2, s_b, r_b, k).start())
+
+    pl.when(z < 7)(lambda: pl.semaphore_wait(later, 4 * (7 - z)))
+
+    @pl.when(owner)
+    def _():
+        cells(lambda at: cell_copy(at).start(), lambda w: w > z)
+        for k in (4, 3, 5, 2, 6, 1, 7):
+            pl.when(mod(z + k, 8) > z)(lambda: z_send(buf2, s_b, r_b, k).start())
+
+    loop(first_pairs, second_pairs, local)
 
     def level_one():
         keys = buf1[:, 0:PICK].reshape(8 * PICK, LANES)
@@ -353,6 +341,29 @@
         for k in range(1, 8):
             ret_send(ret1, got1, s_e, r_e, k).start()
         got1[pair] = ret1[i]
+
+    @pl.when(owner)
+    def _():
+        for k in range(1, 32):
+            at = mod(cell + k, 32)
+            copy(all3.at[at], all3.at[at], s_q.at[at], r_q.at[at], at_cell(at)).wait_recv()
+        hot = onehot(iota((16, LANES), 1) == 8 * iota((16, LANES), 0) + 1)
+        queries = nn(hot, ring3[...].reshape(LANES, LANES).astype(BF16)).astype(BF16)
+        rows = all3[...].reshape(TOK, LANES)
+        s = nt(queries, rows)
+        top = jnp.max(s, axis=1, keepdims=True)
+        e = jnp.exp2((s - top) * COEF)
+        total = jnp.sum(e, axis=1, keepdims=True)
+        numer = nn(e.astype(BF16), rows)
+        c = iota((16, LANES), 1)
+        own_half = (c >= HALF) == odd
+        spot = mod(c, HALF)
+        stats = jnp.where(spot == 0, top, jnp.where(spot == 1, total, 0.0))
+        whole = jnp.where(own_half, stats, numer)
+        ret3[...] = jnp.broadcast_to(whole[:, None, :], (16, 8, LANES))
+        for k in range(1, 16):
+            back_copy(k).start()
+        got3[head] = ret3[ring]
 
     def keys_values(buf):
         wide = buf[...].reshape(64, 16, LANES).astype(F32)
@@ -386,7 +397,7 @@
             ret_send(ret2, got2, s_f, r_f, k).start()
         got2[pair] = ret2[i]
 
-    loop(third_pairs, PAIRS, local)
+    loop(second_pairs, PAIRS, local)
 
     for p in range(PAIRS):
         @pl.when(i != p + 1)
@@ -398,25 +409,27 @@
         def _(p=p):
             copy(ret2.at[0], got2.at[p], s_f.at[1], r_f.at[p], (outer, p + 1)).wait_recv()
 
-    for k in range(1, 32):
-        at = mod(cell + k, 32)
-        copy(part3.at[at], got3.at[at], s_p.at[k], r_p.at[at], of_cell(k)).wait_recv()
-    x = got3[...]
-    lane3 = iota((32, 16, LANES), 2)
-    other = mod(iota((32, 16, LANES), 1), 2) != div(lane3, HALF)
-    spot = mod(lane3, HALF)
-    top = jnp.max(jnp.where(jnp.logical_and(other, spot == 0), x, NEG), axis=2, keepdims=True)
-    total = jnp.sum(jnp.where(jnp.logical_and(other, spot == 1), x, 0.0), axis=2, keepdims=True)
-    peak = jnp.max(top, axis=0, keepdims=True)
-    f = jnp.exp2((top - peak) * COEF)
-    numer = jnp.sum(f * x, axis=0)
-    total = jnp.sum(f * total, axis=0)
+    for h in range(2 * PAIRS):
+        pl.when(jnp.logical_not(mine(h)))(
+            lambda: copy(ret3.at[0], got3.at[h], s_p.at[0], r_p.at[h], ring_owner(h)).wait_recv()
+        )
+    at = iota((8, LANES), 0)
+    halves = []
+    for first_head in (0, 8):
+        rows = jnp.zeros((8, LANES), F32)
+        for h in range(first_head, min(first_head + 8, 2 * PAIRS)):
+            rows = jnp.where(at == h - first_head, got3[h], rows)
+        halves.append(rows)
+    x = jnp.concatenate(halves, axis=0)
     r, c = iota((16, LANES), 0), iota((16, LANES), 1)
-    mine = mod(r, 2) == div(c, HALF)
+    own_half = mod(r, 2) == div(c, HALF)
     spot = mod(c, HALF)
-    for n, v in enumerate(split3(peak.reshape(16, 1)) + split3(total)):
-        numer = jnp.where(jnp.logical_and(jnp.logical_not(mine), spot == n), v, numer)
-    rows4 = jnp.where(jnp.logical_or(mine, spot < 6), numer, 0.0).astype(BF16)
+    top = jnp.max(jnp.where(jnp.logical_and(own_half, spot == 0), x, NEG), axis=1, keepdims=True)
+    total = jnp.sum(jnp.where(jnp.logical_and(own_half, spot == 1), x, 0.0), axis=1, keepdims=True)
+    x = jnp.where(own_half, 0.0, x)
+    for n, v in enumerate(split3(top) + split3(total)):
+        x = jnp.where(jnp.logical_and(own_half, spot == n), v, x)
+    rows4 = x.astype(BF16)
     r, c = iota((16, PAIRS * LANES), 0), iota((16, PAIRS * LANES), 1)
     all4 = tn(rows4, onehot(jnp.logical_and(r == div(c, HALF), mod(c, HALF) == 0)))
 
@@ -426,13 +439,13 @@
     on = mod(lane, 8) == 0
     on4 = mod(lane, HALF) == 0
 
-    def unpacked(x):
+    def unpacked(x, first):
         st = jnp.where(first, x[64:72], x[0:8])
         return (st[0:1] + st[1:2]) + st[2:3], (st[3:4] + st[4:5]) + st[5:6], jnp.where(first, x[0:64], x[64:128])
 
     for p in range(PAIRS):
-        top2, total2, numer2 = unpacked(tn(got2[p], hot))
-        top3, total3, numer3 = unpacked(all4[:, cols(p)])
+        top2, total2, numer2 = unpacked(tn(got2[p], hot), first)
+        top3, total3, numer3 = unpacked(all4[:, cols(p)], jnp.logical_not(first))
         y = got1[p].astype(F32)
         numer1 = y[0:64]
         top1 = (y[64:65] + y[65:66]) + y[66:67]
@@ -452,12 +465,8 @@
         back = nt(spread[p], both)
         out_ref[:, cols(p)] = (out_ref[:, cols(p)].astype(F32) + back).astype(BF16)
 
-    for k in range(1, 16):
-        ring_copy(k).wait_send()
-    for k in range(1, 32):
-        query_copy(k).wait_send()
-    for half in range(2):
-        others(half, lambda at: part_copy(at).wait_send())
+    for h in range(2 * PAIRS):
+        pl.when(jnp.logical_not(mine(h)))(lambda: ring_copy(h).wait_send())
     for p in range(PAIRS):
         @pl.when(i != p + 1)
         def _(p=p):
@@ -470,6 +479,9 @@
             z_send(buf2, s_b, r_b, k).wait_send()
             ret_send(ret1, got1, s_e, r_e, k).wait_send()
             ret_send(ret2, got2, s_f, r_f, k).wait_send()
+        cells(lambda at: cell_copy(at).wait_send(), lambda w: w >= 0)
+        for k in range(1, 16):
+            back_copy(k).wait_send()
 
 
 def shards(queries, keys, values, offsets, w_out):
@@ -491,14 +503,15 @@
             pltpu.VMEM((PAIRS, 80, LANES), BF16),
             pltpu.VMEM((8, 16, LANES), BF16),
             pltpu.VMEM((PAIRS, 16, LANES), BF16),
-            pltpu.VMEM((16, 16, LANES), BF16),
-            pltpu.VMEM((32, 8, LANES), F32),
-            pltpu.VMEM((32, 16, LANES), F32),
-            pltpu.VMEM((32, 16, LANES), F32),
+            pltpu.VMEM((2 * PAIRS, 8, LANES), F32),
+            pltpu.VMEM((16, 8, LANES), F32),
+            pltpu.VMEM((32, 16, LANES), BF16),
+            pltpu.VMEM((16, 8, LANES), F32),
+            pltpu.VMEM((2 * PAIRS, 8, LANES), F32),
             pltpu.VMEM((PAIRS, TOK, LANES), BF16),
             pltpu.VMEM((PAIRS, 144, TOK), BF16),
             pltpu.VMEM((PAIRS, 80, LANES), F32),
-        ] + [dma((6,))] + [dma((8,))] * 10 + [dma((16,))] * 2 + [dma((32,))] * 4,
+        ] + [dma((6,))] + [dma((8,))] * 10 + [dma((16,))] * 2 + [dma((32,))] * 4 + [pltpu.SemaphoreType.REGULAR],
         compiler_params=pltpu.CompilerParams(
             collective_id=0, has_side_effects=True, vmem_limit_bytes=53 * 1024 * 1024
         ),

time: 41.2 us -> 40.9 us (level)
  the two profiles are of different devices: /device:TPU:3 before, /device:TPU:1 now
where the time goes in v3:
time: 40.9 us; the launch traced here: 40.7 us
  Pallas kernels  38.3 us (94%)
  matrix products  1.67 us (4%)
  local copies, waits for them, and re-layouts  0.76 us (2%)
    pallas_call x1, Pallas kernels, shards(): pl.pallas_call(kernel, out_shape=jax.ShapeDtypeStruct(queries.shape, BF16...  38.3 us
    dot_general x1, matrix products, shards(): return jnp.dot(attended, w_out, preferred_element_type=F32).astype(BF16)  1.67 us

profile of v3, /device:TPU:1, one launch (start us, length us, event | category | flops | bytes accessed | tf_op | source)
XLA Modules:
  0.0 40.7 jit_solution(14250882266051361327)
XLA Ops:
  0.0 0.0 copy-start
  0.0 0.0 copy-start.1
  0.0 0.7 %copy-done.1 = s32[12]{0:T(128)S(1)} copy-done((s32[12]{0:T(128)S(1)}, s32[12]{0:T(128)}, u32[]{:S(2)}) %copy-start.1) | copy-done | bytes 72
  0.8 38.3 %shard_map.55 = bf16[512,768]{1,0:T(8,128)(2,1)S(1)} custom-call(s32[12]{0:T(128)S(1)} %copy-done.1, bf16[8,64,768]{2,1,0:T(8,128)(2,1)} %bitcast.5, bf16[8,64,768]{2,1,0:T(8,128)(2,1)} %bitcast.6, bf16[8,64,768]{2,1,0:T(8,128)(2,1)} %bitcast.7), custom_call_target="tpu_custom_call" | custom-call | tf_op jit(solution)/shard_map/pallas_call | solution.py:491
  39.0 0.0 copy-done
  39.1 1.7 %convolution_convert_fusion = bf16[512,768]{1,0:T(8,128)(2,1)} fusion(bf16[512,768]{1,0:T(8,128)(2,1)S(1)} %shard_map.55, bf16[768,768]{1,0:T(8,128)(2,1)S(1)} %copy-done), kind=kOutput, calls=%fused_computation | convolution fusion | flops 604372992 | bytes 2752512 | tf_op jit(solution)/shard_map/dot_general | solution.py:519
Async XLA Ops:
  0.0 39.0 %copy-start = (bf16[768,768]{1,0:T(8,128)(2,1)S(1)}, bf16[768,768]{1,0:T(8,128)(2,1)}, u32[]{:S(2)}) copy-start(bf16[768,768]{1,0:T(8,128)(2,1)} %param.9) | copy-start | bytes 3538948
  0.0 0.8 %copy-start.1 = (s32[12]{0:T(128)S(1)}, s32[12]{0:T(128)}, u32[]{:S(2)}) copy-start(s32[12]{0:T(128)} %off_ref.1) | copy-start | bytes 148

commit v4 on v3

--- a/solution.py
+++ b/solution.py
@@ -76,8 +76,8 @@
     return top, nn(v_up, w)
 
 
-def kernel(off_ref, q_hbm, k_hbm, v_hbm, out_ref, q_ref, k_ref, v_ref, k_few, v_few, q_few, pick2, pick1, buf1, buf2,
-           ret1, got1, ret2, got2, rows3, ring3, all3, ret3, got3, spread, v_up, sel_loc, s_in, s_a1, r_a1, s_a2, r_a2, s_b, r_b,
+def kernel(off_hbm, q_hbm, k_hbm, v_hbm, out_ref, q_ref, k_ref, v_ref, k_few, v_few, q_few, pick2, pick1, buf1, buf2,
+           ret1, got1, ret2, got2, rows3, ring3, all3, ret3, got3, spread, v_up, sel_loc, off_ref, s_in, s_a1, r_a1, s_a2, r_a2, s_b, r_b,
            s_e, r_e, s_f, r_f, s_g, r_g, s_q, r_q, s_p, r_p, later):
     outer = lax.axis_index("outer")
     i = lax.axis_index("inner")
@@ -93,6 +93,8 @@
     first_pairs = jnp.clip(7 - z, 1, PAIRS)
     second_pairs = jnp.maximum(first_pairs, 4)
 
+    offsets = pltpu.make_async_copy(off_hbm, off_ref, s_in.at[6])
+    offsets.start()
     loads = [pltpu.make_async_copy(hbm.at[:, pl.ds(0, 16)], few, s_in.at[n])
              for n, (hbm, few) in enumerate(((k_hbm, k_few), (v_hbm, v_few)))]
     loads += [pltpu.make_async_copy(q_hbm.at[0, pl.ds(0, 16)], q_few, s_in.at[2])]
@@ -143,6 +145,7 @@
         return pltpu.make_async_remote_copy(src_ref=src, dst_ref=dst, send_sem=s, recv_sem=r, device_id=to,
                                             device_id_type=MESH)
 
+    offsets.wait()
     for load in loads[:3]:
         load.wait()
 
@@ -302,16 +305,16 @@
         for k in range(1, 8):
             src = mod(i + k, 8)
             copy(pick2.at[0], buf2.at[z, src], s_a1.at[0], r_a1.at[src], of_inner(k)).wait_recv()
-        for k in (4, 3, 5, 2, 6, 1, 7):
-            pl.when(mod(z + k, 8) < z)(lambda: z_send(buf2, s_b, r_b, k).start())
+        for to in range(7):
+            pl.when(to < z)(lambda: z_send(buf2, s_b, r_b, mod(to - z + 8, 8)).start())
 
     pl.when(z < 7)(lambda: pl.semaphore_wait(later, 4 * (7 - z)))
 
     @pl.when(owner)
     def _():
         cells(lambda at: cell_copy(at).start(), lambda w: w > z)
-        for k in (4, 3, 5, 2, 6, 1, 7):
-            pl.when(mod(z + k, 8) > z)(lambda: z_send(buf2, s_b, r_b, k).start())
+        for to in range(1, 8):
+            pl.when(to > z)(lambda: z_send(buf2, s_b, r_b, mod(to - z + 8, 8)).start())
 
     loop(first_pairs, second_pairs, local)
 
@@ -403,6 +406,38 @@
         @pl.when(i != p + 1)
         def _(p=p):
             copy(ret1.at[0], got1.at[p], s_e.at[1], r_e.at[p], (outer, p + 1)).wait_recv()
+
+    for h in range(2 * PAIRS):
+        pl.when(jnp.logical_not(mine(h)))(lambda: ring_copy(h).wait_send())
+    for p in range(PAIRS):
+        @pl.when(i != p + 1)
+        def _(p=p):
+            send_a1(p).wait_send()
+            send_a2(p).wait_send()
+
+    @pl.when(owner)
+    def _():
+        for k in range(1, 8):
+            z_send(buf2, s_b, r_b, k).wait_send()
+            ret_send(ret1, got1, s_e, r_e, k).wait_send()
+            ret_send(ret2, got2, s_f, r_f, k).wait_send()
+        cells(lambda at: cell_copy(at).wait_send(), lambda w: w >= 0)
+        for k in range(1, 16):
+            back_copy(k).wait_send()
+
+    first = lane < HALF
+    for p in range(PAIRS):
+        y = got1[p].astype(F32)
+        top1 = (y[64:65] + y[65:66]) + y[66:67]
+        total1 = (y[67:68] + y[68:69]) + y[69:70]
+        top0 = sel_loc[p, 64:65]
+        peak = jnp.maximum(top0, top1)
+        f0 = jnp.exp2((top0 - peak) * COEF)
+        f1 = jnp.exp2((top1 - peak) * COEF)
+        total = f0 * sel_loc[p, 72:73] + f1 * total1
+        sel_loc[p, 0:64] = f0 * sel_loc[p, 0:64] + f1 * y[0:64]
+        sel_loc[p, 64:72] = jnp.broadcast_to(peak, (8, LANES))
+        sel_loc[p, 72:80] = jnp.broadcast_to(total, (8, LANES))
 
     for p in range(PAIRS):
         @pl.when(i != p + 1)
@@ -435,7 +470,6 @@
 
     r, c = iota((16, LANES), 0), iota((16, LANES), 1)
     hot = onehot(jnp.logical_and(div(r, 8) == div(c, HALF), mod(c, HALF) == 8 * mod(r, 8)))
-    first = lane < HALF
     on = mod(lane, 8) == 0
     on4 = mod(lane, HALF) == 0
 
@@ -446,42 +480,18 @@
     for p in range(PAIRS):
         top2, total2, numer2 = unpacked(tn(got2[p], hot), first)
         top3, total3, numer3 = unpacked(all4[:, cols(p)], jnp.logical_not(first))
-        y = got1[p].astype(F32)
-        numer1 = y[0:64]
-        top1 = (y[64:65] + y[65:66]) + y[66:67]
-        total1 = (y[67:68] + y[68:69]) + y[69:70]
         top0 = sel_loc[p, 64:65]
-        total0 = sel_loc[p, 72:73]
         top2 = jnp.where(on, top2, top0)
         top3 = jnp.where(on4, top3, top0)
-        peak = jnp.maximum(jnp.maximum(top0, top1), jnp.maximum(top2, top3))
+        peak = jnp.maximum(top0, jnp.maximum(top2, top3))
         f0 = jnp.exp2((top0 - peak) * COEF)
-        f1 = jnp.exp2((top1 - peak) * COEF)
         f2 = jnp.where(on, jnp.exp2((top2 - peak) * COEF), 0.0)
         f3 = jnp.where(on4, jnp.exp2((top3 - peak) * COEF), 0.0)
-        total = f0 * total0 + f1 * total1 + f2 * total2 + f3 * total3
-        done = (f0 * sel_loc[p, 0:64] + f1 * numer1 + f2 * numer2 + f3 * numer3) / total
+        total = f0 * sel_loc[p, 72:73] + f2 * total2 + f3 * total3
+        done = (f0 * sel_loc[p, 0:64] + f2 * numer2 + f3 * numer3) / total
         both = jnp.concatenate([jnp.where(first, done, 0.0), jnp.where(first, 0.0, done)], axis=0).astype(BF16)
         back = nt(spread[p], both)
         out_ref[:, cols(p)] = (out_ref[:, cols(p)].astype(F32) + back).astype(BF16)
-
-    for h in range(2 * PAIRS):
-        pl.when(jnp.logical_not(mine(h)))(lambda: ring_copy(h).wait_send())
-    for p in range(PAIRS):
-        @pl.when(i != p + 1)
-        def _(p=p):
-            send_a1(p).wait_send()
-            send_a2(p).wait_send()
-
-    @pl.when(owner)
-    def _():
-        for k in range(1, 8):
-            z_send(buf2, s_b, r_b, k).wait_send()
-            ret_send(ret1, got1, s_e, r_e, k).wait_send()
-            ret_send(ret2, got2, s_f, r_f, k).wait_send()
-        cells(lambda at: cell_copy(at).wait_send(), lambda w: w >= 0)
-        for k in range(1, 16):
-            back_copy(k).wait_send()
 
 
 def shards(queries, keys, values, offsets, w_out):
@@ -491,7 +501,7 @@
     attended = pl.pallas_call(
         kernel,
         out_shape=jax.ShapeDtypeStruct(queries.shape, BF16),
-        in_specs=[pl.BlockSpec(memory_space=pltpu.SMEM), hbm, hbm, hbm],
+        in_specs=[hbm] * 4,
         out_specs=pl.BlockSpec(memory_space=pltpu.VMEM),
         scratch_shapes=[pltpu.VMEM(shape, BF16)] * 3 + [pltpu.VMEM((8, 16, shape[2]), BF16)] * 2 + [
             pltpu.VMEM((16, shape[2]), BF16),
@@ -511,7 +521,8 @@
             pltpu.VMEM((PAIRS, TOK, LANES), BF16),
             pltpu.VMEM((PAIRS, 144, TOK), BF16),
             pltpu.VMEM((PAIRS, 80, LANES), F32),
-        ] + [dma((6,))] + [dma((8,))] * 10 + [dma((16,))] * 2 + [dma((32,))] * 4 + [pltpu.SemaphoreType.REGULAR],
+            pltpu.SMEM(offsets.shape, jnp.int32),
+        ] + [dma((7,))] + [dma((8,))] * 10 + [dma((16,))] * 2 + [dma((32,))] * 4 + [pltpu.SemaphoreType.REGULAR],
         compiler_params=pltpu.CompilerParams(
             collective_id=0, has_side_effects=True, vmem_limit_bytes=53 * 1024 * 1024
         ),

time: 40.9 us -> 38.5 us (0.941)
  Pallas kernels: 38.3 us -> 35.9 us
    pallas_call x1, Pallas kernels: 38.3 us -> 35.9 us  [shards(): pl.pallas_call(kernel, out_shape=jax.ShapeDtypeStruct(queries.shape, BF16...]
where the time goes in v4:
time: 38.5 us; the launch traced here: 38.3 us
  Pallas kernels  35.9 us (93%)
  matrix products  1.67 us (4%)
  local copies, waits for them, and re-layouts  0.76 us (2%)
    pallas_call x1, Pallas kernels, shards(): pl.pallas_call(kernel, out_shape=jax.ShapeDtypeStruct(queries.shape, BF16...  35.9 us
    dot_general x1, matrix products, shards(): return jnp.dot(attended, w_out, preferred_element_type=F32).astype(BF16)  1.67 us

profile of v4, /device:TPU:1, one launch (start us, length us, event | category | flops | bytes accessed | tf_op | source)
XLA Modules:
  0.0 38.3 jit_solution(16039334291175543889)
XLA Ops:
  0.0 0.0 copy-start
  0.0 0.0 copy-start.1
  0.0 0.7 %copy-done.1 = s32[12]{0:T(128)S(1)} copy-done((s32[12]{0:T(128)S(1)}, s32[12]{0:T(128)}, u32[]{:S(2)}) %copy-start.1) | copy-done | bytes 72
  0.8 35.9 %shard_map.55 = bf16[512,768]{1,0:T(8,128)(2,1)S(1)} custom-call(s32[12]{0:T(128)S(1)} %copy-done.1, bf16[8,64,768]{2,1,0:T(8,128)(2,1)} %bitcast.5, bf16[8,64,768]{2,1,0:T(8,128)(2,1)} %bitcast.6, bf16[8,64,768]{2,1,0:T(8,128)(2,1)} %bitcast.7), custom_call_target="tpu_custom_call" | custom-call | tf_op jit(solution)/shard_map/pallas_call | solution.py:501
  36.6 0.0 copy-done
  36.6 1.7 %convolution_convert_fusion = bf16[512,768]{1,0:T(8,128)(2,1)} fusion(bf16[512,768]{1,0:T(8,128)(2,1)S(1)} %shard_map.55, bf16[768,768]{1,0:T(8,128)(2,1)S(1)} %copy-done), kind=kOutput, calls=%fused_computation | convolution fusion | flops 604372992 | bytes 2752512 | tf_op jit(solution)/shard_map/dot_general | solution.py:530
Async XLA Ops:
  0.0 36.6 %copy-start = (bf16[768,768]{1,0:T(8,128)(2,1)S(1)}, bf16[768,768]{1,0:T(8,128)(2,1)}, u32[]{:S(2)}) copy-start(bf16[768,768]{1,0:T(8,128)(2,1)} %param.9) | copy-start | bytes 3538948
  0.0 0.8 %copy-start.1 = (s32[12]{0:T(128)S(1)}, s32[12]{0:T(128)}, u32[]{:S(2)}) copy-start(s32[12]{0:T(128)} %off_hbm.1) | copy-start | bytes 148

commit v5 on v4

--- a/solution.py
+++ b/solution.py
@@ -90,7 +90,7 @@
     odd = mod(head, 2) == 1
     pair = i - 1
     owner = jnp.logical_and(i >= 1, i <= PAIRS)
-    first_pairs = jnp.clip(7 - z, 1, PAIRS)
+    first_pairs = jnp.clip(6 - z, 0, PAIRS)
     second_pairs = jnp.maximum(first_pairs, 4)
 
     offsets = pltpu.make_async_copy(off_hbm, off_ref, s_in.at[6])
@@ -276,14 +276,15 @@
     for p in range(PAIRS):
         select(p)
 
-    for p in range(PAIRS):
-        @pl.when(i != p + 1)
-        def _(p=p):
-            send_a2(p).start()
-
-        @pl.when(i == p + 1)
-        def _(p=p):
-            buf1[i] = pick1[p]
+    def deal():
+        for p in range(PAIRS):
+            pl.when(i != p + 1)(lambda: send_a2(p).start())
+
+            @pl.when(i == p + 1)
+            def _(p=p):
+                buf1[i] = pick1[p]
+
+    pl.when(z < 4)(deal)
 
     def z_send(buf, s, r, k):
         return copy(buf.at[z], buf.at[z], s.at[k], r.at[z], of_z(k))
@@ -308,6 +309,8 @@
         for to in range(7):
             pl.when(to < z)(lambda: z_send(buf2, s_b, r_b, mod(to - z + 8, 8)).start())
 
+    pl.when(z >= 4)(deal)
+
     pl.when(z < 7)(lambda: pl.semaphore_wait(later, 4 * (7 - z)))
 
     @pl.when(owner)
@@ -347,11 +350,11 @@
 
     @pl.when(owner)
     def _():
+        hot = onehot(iota((16, LANES), 1) == 8 * iota((16, LANES), 0) + 1)
+        queries = nn(hot, ring3[...].reshape(LANES, LANES).astype(BF16)).astype(BF16)
         for k in range(1, 32):
             at = mod(cell + k, 32)
             copy(all3.at[at], all3.at[at], s_q.at[at], r_q.at[at], at_cell(at)).wait_recv()
-        hot = onehot(iota((16, LANES), 1) == 8 * iota((16, LANES), 0) + 1)
-        queries = nn(hot, ring3[...].reshape(LANES, LANES).astype(BF16)).astype(BF16)
         rows = all3[...].reshape(TOK, LANES)
         s = nt(queries, rows)
         top = jnp.max(s, axis=1, keepdims=True)
@@ -443,6 +446,25 @@
         @pl.when(i != p + 1)
         def _(p=p):
             copy(ret2.at[0], got2.at[p], s_f.at[1], r_f.at[p], (outer, p + 1)).wait_recv()
+
+    def unpacked(x, first):
+        st = jnp.where(first, x[64:72], x[0:8])
+        return (st[0:1] + st[1:2]) + st[2:3], (st[3:4] + st[4:5]) + st[5:6], jnp.where(first, x[0:64], x[64:128])
+
+    r, c = iota((16, LANES), 0), iota((16, LANES), 1)
+    hot = onehot(jnp.logical_and(div(r, 8) == div(c, HALF), mod(c, HALF) == 8 * mod(r, 8)))
+    on = mod(lane, 8) == 0
+    for p in range(PAIRS):
+        top2, total2, numer2 = unpacked(tn(got2[p], hot), first)
+        top0 = sel_loc[p, 64:65]
+        top2 = jnp.where(on, top2, top0)
+        peak = jnp.maximum(top0, top2)
+        f0 = jnp.exp2((top0 - peak) * COEF)
+        f2 = jnp.where(on, jnp.exp2((top2 - peak) * COEF), 0.0)
+        total = f0 * sel_loc[p, 72:73] + f2 * total2
+        sel_loc[p, 0:64] = f0 * sel_loc[p, 0:64] + f2 * numer2
+        sel_loc[p, 64:72] = jnp.broadcast_to(peak, (8, LANES))
+        sel_loc[p, 72:80] = jnp.broadcast_to(total, (8, LANES))
 
     for h in range(2 * PAIRS):
         pl.when(jnp.logical_not(mine(h)))(
@@ -468,27 +490,17 @@
     r, c = iota((16, PAIRS * LANES), 0), iota((16, PAIRS * LANES), 1)
     all4 = tn(rows4, onehot(jnp.logical_and(r == div(c, HALF), mod(c, HALF) == 0)))
 
-    r, c = iota((16, LANES), 0), iota((16, LANES), 1)
-    hot = onehot(jnp.logical_and(div(r, 8) == div(c, HALF), mod(c, HALF) == 8 * mod(r, 8)))
-    on = mod(lane, 8) == 0
     on4 = mod(lane, HALF) == 0
 
-    def unpacked(x, first):
-        st = jnp.where(first, x[64:72], x[0:8])
-        return (st[0:1] + st[1:2]) + st[2:3], (st[3:4] + st[4:5]) + st[5:6], jnp.where(first, x[0:64], x[64:128])
-
-    for p in range(PAIRS):
-        top2, total2, numer2 = unpacked(tn(got2[p], hot), first)
+    for p in range(PAIRS):
         top3, total3, numer3 = unpacked(all4[:, cols(p)], jnp.logical_not(first))
         top0 = sel_loc[p, 64:65]
-        top2 = jnp.where(on, top2, top0)
         top3 = jnp.where(on4, top3, top0)
-        peak = jnp.maximum(top0, jnp.maximum(top2, top3))
+        peak = jnp.maximum(top0, top3)
         f0 = jnp.exp2((top0 - peak) * COEF)
-        f2 = jnp.where(on, jnp.exp2((top2 - peak) * COEF), 0.0)
         f3 = jnp.where(on4, jnp.exp2((top3 - peak) * COEF), 0.0)
-        total = f0 * sel_loc[p, 72:73] + f2 * total2 + f3 * total3
-        done = (f0 * sel_loc[p, 0:64] + f2 * numer2 + f3 * numer3) / total
+        total = f0 * sel_loc[p, 72:73] + f3 * total3
+        done = (f0 * sel_loc[p, 0:64] + f3 * numer3) / total
         both = jnp.concatenate([jnp.where(first, done, 0.0), jnp.where(first, 0.0, done)], axis=0).astype(BF16)
         back = nt(spread[p], both)
         out_ref[:, cols(p)] = (out_ref[:, cols(p)].astype(F32) + back).astype(BF16)

time: 38.5 us -> 38.3 us (level)
  no operation moved by 1% of the time
where the time goes in v5:
time: 38.3 us; the launch traced here: 38.1 us
  Pallas kernels  35.7 us (93%)
  matrix products  1.67 us (4%)
  local copies, waits for them, and re-layouts  0.76 us (2%)
    pallas_call x1, Pallas kernels, shards(): pl.pallas_call(kernel, out_shape=jax.ShapeDtypeStruct(queries.shape, BF16...  35.7 us
    dot_general x1, matrix products, shards(): return jnp.dot(attended, w_out, preferred_element_type=F32).astype(BF16)  1.67 us

profile of v5, /device:TPU:1, one launch (start us, length us, event | category | flops | bytes accessed | tf_op | source)
XLA Modules:
  0.0 38.1 jit_solution(15115741456497309374)
XLA Ops:
  0.0 0.0 copy-start
  0.0 0.0 copy-start.1
  0.0 0.7 %copy-done.1 = s32[12]{0:T(128)S(1)} copy-done((s32[12]{0:T(128)S(1)}, s32[12]{0:T(128)}, u32[]{:S(2)}) %copy-start.1) | copy-done | bytes 72
  0.8 35.7 %shard_map.55 = bf16[512,768]{1,0:T(8,128)(2,1)S(1)} custom-call(s32[12]{0:T(128)S(1)} %copy-done.1, bf16[8,64,768]{2,1,0:T(8,128)(2,1)} %bitcast.5, bf16[8,64,768]{2,1,0:T(8,128)(2,1)} %bitcast.6, bf16[8,64,768]{2,1,0:T(8,128)(2,1)} %bitcast.7), custom_call_target="tpu_custom_call" | custom-call | tf_op jit(solution)/shard_map/pallas_call | solution.py:513
  36.4 0.0 copy-done
  36.4 1.7 %convolution_convert_fusion = bf16[512,768]{1,0:T(8,128)(2,1)} fusion(bf16[512,768]{1,0:T(8,128)(2,1)S(1)} %shard_map.55, bf16[768,768]{1,0:T(8,128)(2,1)S(1)} %copy-done), kind=kOutput, calls=%fused_computation | convolution fusion | flops 604372992 | bytes 2752512 | tf_op jit(solution)/shard_map/dot_general | solution.py:542
Async XLA Ops:
  0.0 36.4 %copy-start = (bf16[768,768]{1,0:T(8,128)(2,1)S(1)}, bf16[768,768]{1,0:T(8,128)(2,1)}, u32[]{:S(2)}) copy-start(bf16[768,768]{1,0:T(8,128)(2,1)} %param.9) | copy-start | bytes 3538948
  0.0 0.8 %copy-start.1 = (s32[12]{0:T(128)S(1)}, s32[12]{0:T(128)}, u32[]{:S(2)}) copy-start(s32[12]{0:T(128)} %off_hbm.1) | copy-start | bytes 148
